TPU v7x, 32 devices: a whole 2x2x4 slice. The times are simulated.
32 devices in a mesh: dp: 16 (over z, y, core), fsdp: 2 (over x).
Axes of the slice: x: 2, y: 2, z: 4, core: 2. Of those that a mesh axis runs over, the one named last changes fastest.
Arguments:
- frames: bfloat16 [4096, 1024], P(('dp', 'fsdp')), may hold values from -6 to 6
- lengths: int32 [32, 4], P(('dp', 'fsdp')), may hold values from 1 to 80, 112 in all within a row
- cotangent: bfloat16 [4096, 1024], P(('dp', 'fsdp')), may hold values from -6 to 6
- conv_kernel: bfloat16 [1024, 8192], P(('dp', 'fsdp')), may hold values from -0.125 to 0.125
- conv_bias: bfloat16 [1024], P(('dp', 'fsdp')), may hold values from -1.75 to 1.75
- norm_one_gain: bfloat16 [1024], P(('dp', 'fsdp')), may hold values from 0.5 to 1.5
- norm_one_bias: bfloat16 [1024], P(('dp', 'fsdp')), may hold values from -1.75 to 1.75
- query_weight: bfloat16 [1024, 1024], P(('dp', 'fsdp')), may hold values from -0.25 to 0.25
- query_bias: bfloat16 [1024], P(('dp', 'fsdp')), may hold values from -3 to 3
- key_weight: bfloat16 [1024, 1024], P(('dp', 'fsdp')), may hold values from -0.25 to 0.25
- value_weight: bfloat16 [1024, 1024], P(('dp', 'fsdp')), may hold values from -0.1875 to 0.1875
- value_bias: bfloat16 [1024], P(('dp', 'fsdp')), may hold values from -1.75 to 1.75
- out_weight: bfloat16 [1024, 1024], P(('dp', 'fsdp')), may hold values from -0.5 to 0.5
- out_bias: bfloat16 [1024], P(('dp', 'fsdp')), may hold values from -1.75 to 1.75
- norm_two_gain: bfloat16 [1024], P(('dp', 'fsdp')), may hold values from 0.5 to 1.5
- norm_two_bias: bfloat16 [1024], P(('dp', 'fsdp')), may hold values from -1.75 to 1.75
- up_weight: bfloat16 [1024, 4096], P(('dp', 'fsdp')), may hold values from -0.1875 to 0.1875
- up_bias: bfloat16 [4096], P(('dp', 'fsdp')), may hold values from -1.75 to 1.75
- down_weight: bfloat16 [4096, 1024], P(('dp', 'fsdp')), may hold values from -0.09375 to 0.09375
- down_bias: bfloat16 [1024], P(('dp', 'fsdp')), may hold values from -1.75 to 1.75
Outputs:
- output: bfloat16 [4096, 1024], P(('dp', 'fsdp'))
- frames_grad: float32 [4096, 1024], P(('dp', 'fsdp'))
- conv_kernel_grad: float32 [1024, 8192], P(('dp', 'fsdp'))
- conv_bias_grad: float32 [1024], P(('dp', 'fsdp'))
- norm_one_gain_grad: float32 [1024], P(('dp', 'fsdp'))
- norm_one_bias_grad: float32 [1024], P(('dp', 'fsdp'))
- query_weight_grad: float32 [1024, 1024], P(('dp', 'fsdp'))
- query_bias_grad: float32 [1024], P(('dp', 'fsdp'))
- key_weight_grad: float32 [1024, 1024], P(('dp', 'fsdp'))
- value_weight_grad: float32 [1024, 1024], P(('dp', 'fsdp'))
- value_bias_grad: float32 [1024], P(('dp', 'fsdp'))
- out_weight_grad: float32 [1024, 1024], P(('dp', 'fsdp'))
- out_bias_grad: float32 [1024], P(('dp', 'fsdp'))
- norm_two_gain_grad: float32 [1024], P(('dp', 'fsdp'))
- norm_two_bias_grad: float32 [1024], P(('dp', 'fsdp'))
- up_weight_grad: float32 [1024, 4096], P(('dp', 'fsdp'))
- up_bias_grad: float32 [4096], P(('dp', 'fsdp'))
- down_weight_grad: float32 [4096, 1024], P(('dp', 'fsdp'))
- down_bias_grad: float32 [1024], P(('dp', 'fsdp'))
Inputs may be any that keep to these rules, and one draw needn't show every extreme that they name: `lengths`: row j lists the utterances of frame block j from its first slot on; they fill the first 112 slots, the rest is padding, and the longest is exactly 80.
All inputs are finite; a program needn't handle non-finite values.
Results may differ from a plain program's by a relative error of at most 0.015.
Values may be sent and summed in bfloat16 or wider, within the bound.
No kernel may reach another device: no remote copies, remote signals or barrier semaphores. Data moves between devices by JAX's collectives and lax.ppermute only.
A program may use at most 512 MiB of HBM per device.

v0:
```python
import functools

import jax
import jax.numpy as jnp
import numpy as np
from jax import lax
from jax.experimental import pallas as pl
from jax.experimental.pallas import tpu as pltpu
from jax.sharding import Mesh
from jax.sharding import PartitionSpec as P

HEAD_DIM = 64
GROUPS = 16
KW = 128


norm_eps = 1e-05
score_scale = 0.125


def layer_norm(rows, scale_vec, shift_vec):
    row_mean = jnp.mean(rows, axis=-1, keepdims=True)
    centred = rows - row_mean
    spread = jnp.mean(centred * centred, axis=-1, keepdims=True)
    return centred * lax.rsqrt(spread + norm_eps) * scale_vec + shift_vec


def gelu_exact(values):
    return jax.nn.gelu(values, approximate=False)


def unfold(source, segment, first_tap, tap_count, flipped):
    rows_count, model_width = source.shape
    half_width = KW // 2
    channels = model_width // GROUPS
    padded = jnp.pad(source, ((half_width, half_width), (0, 0))).reshape(
        rows_count + KW, GROUPS, channels
    )
    seg_padded = jnp.pad(segment, (half_width, half_width), constant_values=-1)
    offsets = [
        KW - tap_index if flipped else tap_index
        for tap_index in range(first_tap, first_tap + tap_count)
    ]
    shifted = jnp.stack([padded[offset : offset + rows_count] for offset in offsets], axis=2)
    same_seg = jnp.stack(
        [seg_padded[offset : offset + rows_count] == segment for offset in offsets], axis=1
    )
    kept_taps = jnp.where(same_seg[:, None, :, None], shifted, jnp.zeros((), source.dtype))
    return kept_taps.reshape(rows_count, GROUPS, tap_count * channels)


def conv_forward(source, segment, conv_kernel):
    rows_count, model_width = source.shape
    channels = model_width // GROUPS
    tap_count = KW // 8
    summed = jnp.zeros((rows_count, GROUPS, channels), jnp.float32)
    for block_index in range(8):
        first_tap = block_index * tap_count
        unfolded = unfold(source, segment, first_tap, tap_count, False)
        kernel_block = conv_kernel[:, first_tap * channels : (first_tap + tap_count) * channels]
        kernel_block = kernel_block.reshape(GROUPS, channels, tap_count * channels)
        summed = summed + jnp.einsum(
            "tgi,goi->tgo", unfolded, kernel_block, preferred_element_type=jnp.float32
        )
    return summed.reshape(rows_count, model_width)


def conv_backward(source, segment, conv_kernel, grad_low):
    rows_count, model_width = source.shape
    channels = model_width // GROUPS
    tap_count = KW // 8
    grad_groups = grad_low.reshape(rows_count, GROUPS, channels)
    kernel_pieces = []
    input_grad = jnp.zeros((rows_count, GROUPS, channels), jnp.float32)
    for block_index in range(8):
        first_tap = block_index * tap_count
        unfolded = unfold(source, segment, first_tap, tap_count, False)
        kernel_term = jnp.einsum(
            "tgo,tgi->goi", grad_groups, unfolded, preferred_element_type=jnp.float32
        )
        kernel_pieces.append(kernel_term.reshape(model_width, tap_count * channels))
        turned = unfold(grad_low, segment, first_tap, tap_count, True).reshape(
            rows_count, GROUPS, tap_count, channels
        )
        kernel_block = conv_kernel[:, first_tap * channels : (first_tap + tap_count) * channels]
        kernel_block = kernel_block.reshape(GROUPS, channels, tap_count, channels)
        input_grad = input_grad + jnp.einsum(
            "tgko,gokc->tgc", turned, kernel_block, preferred_element_type=jnp.float32
        )
    return (kernel_pieces, input_grad.reshape(rows_count, model_width))


def sum_kernel_half(piece):
    return lax.psum_scatter(piece, ("dp", "fsdp"), scatter_dimension=0, tiled=True)


def attention_scores(query_h, key_h, related):
    scores = (
        jnp.einsum("qhd,khd->hqk", query_h, key_h, preferred_element_type=jnp.float32) * score_scale
    )
    return jnp.where(related[None], scores, -1000000000.0)


def local_plain(
    frames,
    lengths,
    cotangent,
    conv_kernel,
    conv_bias,
    norm_one_gain,
    norm_one_bias,
    query_weight,
    query_bias,
    key_weight,
    value_weight,
    value_bias,
    out_weight,
    out_bias,
    norm_two_gain,
    norm_two_bias,
    up_weight,
    up_bias,
    down_weight,
    down_bias,
):
    rows_count, model_width = frames.shape
    head_count = model_width // HEAD_DIM
    ends = jnp.cumsum(lengths[0])
    positions = lax.broadcasted_iota(jnp.int32, (rows_count, ends.shape[0]), 0)
    segment = jnp.sum((positions >= ends[None, :]).astype(jnp.int32), axis=1)
    valid = (segment < ends.shape[0]).astype(jnp.float32)
    related = segment[:, None] == segment[None, :]
    conv_set = (conv_kernel, conv_bias, norm_one_gain, norm_one_bias)
    attn_set = (
        query_weight,
        key_weight,
        value_weight,
        out_weight,
        query_bias,
        value_bias,
        out_bias,
    )
    ffn_set = (up_weight, down_weight, up_bias, down_bias, norm_two_gain, norm_two_bias)
    source_f = frames.astype(jnp.float32)
    conv_full = (
        lax.all_gather(conv_set[0], ("dp", "fsdp"), axis=0, tiled=True),
        lax.all_gather(conv_set[1], ("dp", "fsdp"), axis=0, tiled=True),
        lax.all_gather(conv_set[2], ("dp", "fsdp"), axis=0, tiled=True),
        lax.all_gather(conv_set[3], ("dp", "fsdp"), axis=0, tiled=True),
    )
    kernel_full, conv_bias_full, gain_one, shift_one = conv_full
    conv_act = conv_forward(frames, segment, kernel_full) + conv_bias_full.astype(jnp.float32)
    conv_gelu, conv_pull = jax.vjp(gelu_exact, conv_act)
    hidden_zero = source_f + conv_gelu
    normed_one, norm_one_pull = jax.vjp(
        layer_norm, hidden_zero, gain_one.astype(jnp.float32), shift_one.astype(jnp.float32)
    )
    normed_one_low = normed_one.astype(jnp.bfloat16)
    attn_full = (
        lax.all_gather(attn_set[0], ("dp", "fsdp"), axis=0, tiled=True),
        lax.all_gather(attn_set[1], ("dp", "fsdp"), axis=0, tiled=True),
        lax.all_gather(attn_set[2], ("dp", "fsdp"), axis=0, tiled=True),
        lax.all_gather(attn_set[3], ("dp", "fsdp"), axis=0, tiled=True),
        lax.all_gather(attn_set[4], ("dp", "fsdp"), axis=0, tiled=True),
        lax.all_gather(attn_set[5], ("dp", "fsdp"), axis=0, tiled=True),
        lax.all_gather(attn_set[6], ("dp", "fsdp"), axis=0, tiled=True),
    )
    query_full, key_full, value_full, out_full, query_bias_full, value_bias_full, out_bias_full = (
        attn_full
    )
    query_low = (
        jnp.dot(normed_one_low, query_full, preferred_element_type=jnp.float32)
        + query_bias_full.astype(jnp.float32)
    ).astype(jnp.bfloat16)
    key_low = jnp.dot(normed_one_low, key_full, preferred_element_type=jnp.float32).astype(
        jnp.bfloat16
    )
    value_low = (
        jnp.dot(normed_one_low, value_full, preferred_element_type=jnp.float32)
        + value_bias_full.astype(jnp.float32)
    ).astype(jnp.bfloat16)
    query_h = query_low.reshape(rows_count, head_count, HEAD_DIM)
    key_h = key_low.reshape(rows_count, head_count, HEAD_DIM)
    value_h = value_low.reshape(rows_count, head_count, HEAD_DIM)
    scores = attention_scores(query_h, key_h, related)
    row_top = jnp.max(scores, axis=-1, keepdims=True)
    expd = jnp.exp(scores - row_top)
    row_total = jnp.sum(expd, axis=-1, keepdims=True)
    probs = expd / row_total
    logsum = row_top + jnp.log(row_total)
    mixed = jnp.einsum(
        "hqk,khd->qhd", probs.astype(jnp.bfloat16), value_h, preferred_element_type=jnp.float32
    )
    mixed_low = mixed.reshape(rows_count, model_width).astype(jnp.bfloat16)
    hidden_one = (
        hidden_zero
        + jnp.dot(mixed_low, out_full, preferred_element_type=jnp.float32)
        + out_bias_full.astype(jnp.float32)
    )
    ffn_full = (
        lax.all_gather(ffn_set[0], ("dp", "fsdp"), axis=0, tiled=True),
        lax.all_gather(ffn_set[1], ("dp", "fsdp"), axis=0, tiled=True),
        lax.all_gather(ffn_set[2], ("dp", "fsdp"), axis=0, tiled=True),
        lax.all_gather(ffn_set[3], ("dp", "fsdp"), axis=0, tiled=True),
        lax.all_gather(ffn_set[4], ("dp", "fsdp"), axis=0, tiled=True),
        lax.all_gather(ffn_set[5], ("dp", "fsdp"), axis=0, tiled=True),
    )
    up_full, down_full, up_bias_full, down_bias_full, gain_two, shift_two = ffn_full
    normed_two, norm_two_pull = jax.vjp(
        layer_norm, hidden_one, gain_two.astype(jnp.float32), shift_two.astype(jnp.float32)
    )
    normed_two_low = normed_two.astype(jnp.bfloat16)
    up_pre = jnp.dot(
        normed_two_low, up_full, preferred_element_type=jnp.float32
    ) + up_bias_full.astype(jnp.float32)
    activated, gelu_pull = jax.vjp(gelu_exact, up_pre)
    activated_low = activated.astype(jnp.bfloat16)
    hidden_two = (
        hidden_one
        + jnp.dot(activated_low, down_full, preferred_element_type=jnp.float32)
        + down_bias_full.astype(jnp.float32)
    )
    output = hidden_two.astype(jnp.bfloat16)
    ffn_back = (
        lax.all_gather(ffn_set[0], ("dp", "fsdp"), axis=0, tiled=True),
        lax.all_gather(ffn_set[1], ("dp", "fsdp"), axis=0, tiled=True),
        lax.all_gather(ffn_set[2], ("dp", "fsdp"), axis=0, tiled=True),
        lax.all_gather(ffn_set[3], ("dp", "fsdp"), axis=0, tiled=True),
        lax.all_gather(ffn_set[4], ("dp", "fsdp"), axis=0, tiled=True),
        lax.all_gather(ffn_set[5], ("dp", "fsdp"), axis=0, tiled=True),
    )
    up_back, down_back = (ffn_back[0], ffn_back[1])
    grad_out = cotangent.astype(jnp.float32) * valid[:, None]
    grad_out_low = grad_out.astype(jnp.bfloat16)
    down_weight_term = jnp.einsum(
        "tf,td->fd", activated_low, grad_out_low, preferred_element_type=jnp.float32
    )
    down_bias_term = jnp.sum(grad_out, axis=0)
    down_sums = (
        lax.psum_scatter(down_weight_term, ("dp", "fsdp"), scatter_dimension=0, tiled=True),
        lax.psum_scatter(down_bias_term, ("dp", "fsdp"), scatter_dimension=0, tiled=True),
    )
    act_grad = jnp.einsum("td,fd->tf", grad_out_low, down_back, preferred_element_type=jnp.float32)
    up_grad = gelu_pull(act_grad)[0]
    up_grad_low = up_grad.astype(jnp.bfloat16)
    up_bias_term = jnp.sum(up_grad, axis=0)
    up_weight_term = jnp.einsum(
        "td,tf->df", normed_two_low, up_grad_low, preferred_element_type=jnp.float32
    )
    normed_two_grad = jnp.einsum(
        "tf,df->td", up_grad_low, up_back, preferred_element_type=jnp.float32
    )
    norm_two_input, gain_two_term, shift_two_term = norm_two_pull(normed_two_grad)
    hidden_one_grad = grad_out + norm_two_input
    up_sums = (
        lax.psum_scatter(up_weight_term, ("dp", "fsdp"), scatter_dimension=0, tiled=True),
        lax.psum_scatter(up_bias_term, ("dp", "fsdp"), scatter_dimension=0, tiled=True),
        lax.psum_scatter(gain_two_term, ("dp", "fsdp"), scatter_dimension=0, tiled=True),
        lax.psum_scatter(shift_two_term, ("dp", "fsdp"), scatter_dimension=0, tiled=True),
    )
    attn_back = (
        lax.all_gather(attn_set[0], ("dp", "fsdp"), axis=0, tiled=True),
        lax.all_gather(attn_set[1], ("dp", "fsdp"), axis=0, tiled=True),
        lax.all_gather(attn_set[2], ("dp", "fsdp"), axis=0, tiled=True),
        lax.all_gather(attn_set[3], ("dp", "fsdp"), axis=0, tiled=True),
        lax.all_gather(attn_set[4], ("dp", "fsdp"), axis=0, tiled=True),
        lax.all_gather(attn_set[5], ("dp", "fsdp"), axis=0, tiled=True),
        lax.all_gather(attn_set[6], ("dp", "fsdp"), axis=0, tiled=True),
    )
    query_back, key_back, value_back, out_back = (
        attn_back[0],
        attn_back[1],
        attn_back[2],
        attn_back[3],
    )
    attn_grad_low = hidden_one_grad.astype(jnp.bfloat16)
    out_bias_term = jnp.sum(hidden_one_grad, axis=0)
    out_weight_term = jnp.einsum(
        "tc,td->cd", mixed_low, attn_grad_low, preferred_element_type=jnp.float32
    )
    mixed_grad = jnp.einsum(
        "td,cd->tc", attn_grad_low, out_back, preferred_element_type=jnp.float32
    ).astype(jnp.bfloat16)
    mixed_grad_h = mixed_grad.reshape(rows_count, head_count, HEAD_DIM)
    probs_again = jnp.exp(attention_scores(query_h, key_h, related) - logsum)
    prob_grad = jnp.einsum(
        "qhd,khd->hqk", mixed_grad_h, value_h, preferred_element_type=jnp.float32
    )
    value_grad = jnp.einsum(
        "hqk,qhd->khd",
        probs_again.astype(jnp.bfloat16),
        mixed_grad_h,
        preferred_element_type=jnp.float32,
    )
    score_grad = probs_again * (
        prob_grad - jnp.sum(probs_again * prob_grad, axis=-1, keepdims=True)
    )
    score_low = score_grad.astype(jnp.bfloat16)
    query_grad = (
        jnp.einsum("hqk,khd->qhd", score_low, key_h, preferred_element_type=jnp.float32)
        * score_scale
    ).reshape(rows_count, model_width)
    key_grad = (
        jnp.einsum("hqk,qhd->khd", score_low, query_h, preferred_element_type=jnp.float32)
        * score_scale
    ).reshape(rows_count, model_width)
    value_grad = value_grad.reshape(rows_count, model_width)
    query_bias_term = jnp.sum(query_grad, axis=0)
    value_bias_term = jnp.sum(value_grad, axis=0)
    query_grad_low = query_grad.astype(jnp.bfloat16)
    key_grad_low = key_grad.astype(jnp.bfloat16)
    value_grad_low = value_grad.astype(jnp.bfloat16)
    query_weight_term = jnp.einsum(
        "tc,td->cd", normed_one_low, query_grad_low, preferred_element_type=jnp.float32
    )
    key_weight_term = jnp.einsum(
        "tc,td->cd", normed_one_low, key_grad_low, preferred_element_type=jnp.float32
    )
    value_weight_term = jnp.einsum(
        "tc,td->cd", normed_one_low, value_grad_low, preferred_element_type=jnp.float32
    )
    normed_one_grad = jnp.einsum(
        "td,cd->tc", query_grad_low, query_back, preferred_element_type=jnp.float32
    )
    normed_one_grad = normed_one_grad + jnp.einsum(
        "td,cd->tc", key_grad_low, key_back, preferred_element_type=jnp.float32
    )
    normed_one_grad = normed_one_grad + jnp.einsum(
        "td,cd->tc", value_grad_low, value_back, preferred_element_type=jnp.float32
    )
    norm_one_input, gain_one_term, shift_one_term = norm_one_pull(normed_one_grad)
    hidden_zero_grad = hidden_one_grad + norm_one_input
    conv_grad = conv_pull(hidden_zero_grad)[0]
    conv_bias_term = jnp.sum(conv_grad, axis=0)
    conv_grad_low = conv_grad.astype(jnp.bfloat16)
    attn_sums = (
        lax.psum_scatter(query_weight_term, ("dp", "fsdp"), scatter_dimension=0, tiled=True),
        lax.psum_scatter(key_weight_term, ("dp", "fsdp"), scatter_dimension=0, tiled=True),
        lax.psum_scatter(value_weight_term, ("dp", "fsdp"), scatter_dimension=0, tiled=True),
        lax.psum_scatter(out_weight_term, ("dp", "fsdp"), scatter_dimension=0, tiled=True),
        lax.psum_scatter(query_bias_term, ("dp", "fsdp"), scatter_dimension=0, tiled=True),
        lax.psum_scatter(value_bias_term, ("dp", "fsdp"), scatter_dimension=0, tiled=True),
        lax.psum_scatter(out_bias_term, ("dp", "fsdp"), scatter_dimension=0, tiled=True),
        lax.psum_scatter(conv_bias_term, ("dp", "fsdp"), scatter_dimension=0, tiled=True),
        lax.psum_scatter(gain_one_term, ("dp", "fsdp"), scatter_dimension=0, tiled=True),
        lax.psum_scatter(shift_one_term, ("dp", "fsdp"), scatter_dimension=0, tiled=True),
    )
    conv_back = (
        lax.all_gather(conv_set[0], ("dp", "fsdp"), axis=0, tiled=True),
        lax.all_gather(conv_set[1], ("dp", "fsdp"), axis=0, tiled=True),
        lax.all_gather(conv_set[2], ("dp", "fsdp"), axis=0, tiled=True),
        lax.all_gather(conv_set[3], ("dp", "fsdp"), axis=0, tiled=True),
    )
    kernel_pieces, frames_conv_grad = conv_backward(frames, segment, conv_back[0], conv_grad_low)
    kernel_halves = []
    for half_index in range(2):
        half_term = jnp.concatenate(kernel_pieces[half_index * 4 : (half_index + 1) * 4], axis=1)
        kernel_halves.append(sum_kernel_half(half_term))
    kernel_grad_out = jnp.concatenate(kernel_halves, axis=1)
    frames_grad = hidden_zero_grad + frames_conv_grad
    return (
        output,
        frames_grad,
        kernel_grad_out,
        attn_sums[7],
        attn_sums[8],
        attn_sums[9],
        attn_sums[0],
        attn_sums[4],
        attn_sums[1],
        attn_sums[2],
        attn_sums[5],
        attn_sums[3],
        attn_sums[6],
        up_sums[2],
        up_sums[3],
        up_sums[0],
        up_sums[1],
        down_sums[0],
        down_sums[1],
    )


NT = (((1,), (1,)), ((), ()))
TN = (((0,), (0,)), ((), ()))
BF, F32 = jnp.bfloat16, jnp.float32


def f32(v):
    return v.astype(jnp.float32)


def low(v):
    return v.astype(jnp.bfloat16)


def dot(a, b):
    return jnp.dot(a, b, preferred_element_type=jnp.float32)


def dot_nt(a, b):
    return lax.dot_general(a, b, NT, preferred_element_type=jnp.float32)


def dot_tn(a, b):
    return lax.dot_general(a, b, TN, preferred_element_type=jnp.float32)


SMEM = pl.BlockSpec(memory_space=pltpu.SMEM)
VMEM = pl.BlockSpec(memory_space=pltpu.VMEM)
ANY = pl.BlockSpec(memory_space=pl.ANY)
HBM = pl.BlockSpec(memory_space=pltpu.HBM)


def shape(dims, dtype=BF):
    return jax.ShapeDtypeStruct(dims, dtype)


def in_hbm(v):
    return pltpu.with_memory_space_constraint(v, pltpu.HBM)


def out_hbm(v):
    return pltpu.HBM(v.shape, v.dtype)


def estimate(cost):
    return pl.CostEstimate(flops=int(cost * 1e9), bytes_accessed=1 << 10, transcendentals=0)


def tie(v, *after):
    def body(*refs):
        pass

    return pl.pallas_call(
        body,
        in_specs=[ANY] * (1 + len(after)),
        out_specs=ANY,
        out_shape=shape(v.shape, v.dtype),
        input_output_aliases={0: 0},
        cost_estimate=estimate(0.1),
    )(v, *after)


def run_copies(plan, sems):
    copies = [pltpu.make_async_copy(a, b, sems.at[i]) for i, (a, b) in enumerate(plan)]
    for copy in copies:
        copy.start()
    for copy in copies:
        copy.wait()


def whole_call(kernel, ins, in_specs, outs, out_specs, scratch=(), cost=0.05, after=(), plan=None, vmem=12):
    many = isinstance(outs, (list, tuple))
    out_list, out_specs = (list(outs), list(out_specs)) if many else ([outs], [out_specs])
    staged_in = [i for i, sp in enumerate(in_specs) if sp is None]
    staged_out = [i for i, sp in enumerate(out_specs) if sp is None]
    stages = [pltpu.VMEM(ins[i].shape, ins[i].dtype) for i in staged_in]
    stages += [pltpu.VMEM(out_list[i].shape, out_list[i].dtype) for i in staged_out]
    n_in, n_out, n_stage = len(ins), len(out_list), len(stages)

    def body(*refs):
        given, made = list(refs[:n_in]), list(refs[n_in + len(after) : n_in + len(after) + n_out])
        rest = refs[n_in + len(after) + n_out :]
        stage, own, sems = rest[:n_stage], rest[n_stage:-1], rest[-1]
        first, last = [], []
        for ref, i in zip(stage, staged_in):
            first.append((given[i], ref))
            given[i] = ref
        for ref, i in zip(stage[len(staged_in) :], staged_out):
            last.append((ref, made[i]))
            made[i] = ref
        groups = plan(*given, *made, *own) if plan is not None else []
        copies = [pltpu.make_async_copy(a, b, sems.at[i]) for i, (a, b) in enumerate(first + sum(groups, []))]
        for copy in copies:
            copy.start()
        for copy in copies[: len(first)]:
            copy.wait()
        ends = [len(first) + sum(len(g) for g in groups[:i]) for i in range(len(groups) + 1)]

        def ready(group):
            for copy in copies[ends[group] : ends[group + 1]]:
                copy.wait()

        kernel(*given, *made, *own, *([ready] if groups else []))
        run_copies(last, sems)

    result = pl.pallas_call(
        body,
        in_specs=[HBM if sp is None else sp for sp in in_specs] + [ANY] * len(after),
        out_specs=[HBM if sp is None else sp for sp in out_specs],
        out_shape=[out_hbm(v) if sp is None else pltpu.VMEM(v.shape, v.dtype) if sp is VMEM else v for v, sp in zip(out_list, out_specs)],
        scratch_shapes=stages + list(scratch) + [pltpu.SemaphoreType.DMA((64,))],
        compiler_params=pltpu.CompilerParams(vmem_limit_bytes=vmem << 20),
        cost_estimate=estimate(cost),
    )(*[in_hbm(v) if sp is None or sp is ANY else v for v, sp in zip(ins, in_specs)], *after)
    return result if many else result[0]


def left(dims):
    return lax.broadcasted_iota(jnp.int32, dims, 1) < 64


def turn(v):
    return pltpu.roll(v, 64, 1)


def cross(a, b):
    lo = left(a.shape)
    return jnp.where(lo, a, turn(b)), jnp.where(lo, turn(a), b)


def pack_kernel(f_ref, s_ref, o_ref):
    small = low(s_ref[...])
    for g in range(8):
        tile = slice(128 * g, 128 * g + 128)
        p, q = cross(f32(f_ref[0:64, tile]), f32(f_ref[64:128, tile]))
        o_ref[2 * g, 0:64, :] = low(p)
        o_ref[2 * g + 1, 0:64, :] = low(q)
    for g in range(16):
        o_ref[g, 64:80, :] = small


def first_kernel(lens_ref, *refs):
    vectors, bias_ref = refs[0:9], refs[9]
    q_ref, k_ref, v_ref, o_ref, mine_ref, theirs_ref, out_ref, small_ref = refs[10:18]
    c = lax.axis_index("c")
    for j, ref in enumerate((q_ref, k_ref, v_ref)):
        for t in range(4):
            even, odd = cross(f32(ref[:, 256 * t : 256 * t + 128]), f32(ref[:, 256 * t + 128 : 256 * t + 256]))
            tile = slice(128 * t, 128 * t + 128)
            mine_ref[j, :, tile] = low(jnp.where(c == 0, even, odd))
            theirs_ref[j, :, tile] = low(jnp.where(c == 0, odd, even))
    for h in range(2):
        out_ref[h] = o_ref[:, 512 * h : 512 * h + 512]
    small_ref[...] = jnp.zeros_like(small_ref)
    for i, ref in enumerate(vectors):
        small_ref[i : i + 1, 0:32] = f32(ref[...]).reshape(1, 32)
    bias = f32(bias_ref[...]).reshape(1, 128)
    lane = lax.broadcasted_iota(jnp.int32, (1, 128), 1)
    for k in range(4):
        row = pltpu.roll(bias, 128 - 32 * k, 1) if k else bias
        small_ref[9 + k : 10 + k, :] = jnp.where(lane < 32, row, 0.0)
    small_ref[13:14, 0:4] = lens_ref[...].astype(jnp.float32)


def ffn_prep_kernel(lens_ref, u_ref, cot_ref, up_ref, g_ref, g_send_ref):
    valid = jnp.sum(lens_ref[...], axis=1, keepdims=True)
    for z in range(4):
        for k in range(8):
            at = 128 * (8 * z + k)
            up_ref[k, :, 128 * z : 128 * z + 128] = u_ref[:, at : at + 128]
    slot = lax.broadcasted_iota(jnp.int32, (128, 1024), 0)
    g_ref[...] = jnp.where(slot < valid, cot_ref[...], jnp.zeros_like(cot_ref))
    g_send_ref[...] = g_ref[...]


def vector_kernel(meta_ref, mine_ref, theirs_ref, vec_ref, up_ref, qv_ref):
    c, x = meta_ref[3], meta_ref[2]
    lane = lax.broadcasted_iota(jnp.int32, (16, 128), 1)
    tiles = []
    for t in range(8):
        tile = jnp.zeros((16, 128), jnp.float32)
        for k in range(4):
            part = jnp.where(x == k % 2, f32(mine_ref[2 * t + k // 2]), f32(theirs_ref[2 * t + k // 2]))
            tile = jnp.where(lane // 32 == k, pltpu.roll(part, 32 * k, 1) if k else part, tile)
        tiles.append(tile)
        vec_ref[:, 128 * t : 128 * t + 128] = tile
    for z in range(4):
        own = jnp.where(meta_ref[1] == 0, tiles[2 * z], tiles[2 * z + 1])
        own = jnp.where(c == 0, own, turn(own))
        own = jnp.where(x == 0, own, pltpu.roll(own, 96, 1))
        up = own[9:10, :]
        for k in range(1, 4):
            up = jnp.where(lane[0:1] // 32 == k, pltpu.roll(own[9 + k : 10 + k, :], 32 * k, 1), up)
        up_ref[0:1, 128 * z : 128 * z + 128] = up
    for t in range(4):
        even, odd = cross(tiles[2 * t], tiles[2 * t + 1])
        qv_ref[:, 128 * t : 128 * t + 128] = jnp.where(c == 0, even, odd)[3:5]


NB = 4
GROUP = 2
ROWS = 208


def starts_of(lens_ref, block):
    starts = [jnp.int32(0)]
    for i in range(4):
        starts.append(starts[-1] + lens_ref[block * 4 + i])
    return starts + [jnp.int32(128)]


def spread(block, starts, buf, out):
    v = f32(block)
    turned, lo = turn(v), left((64, 128))
    buf[80:144, :] = jnp.where(lo, v, turned)
    buf[144:208, :] = jnp.where(lo, turned, v)
    row = lax.broadcasted_iota(jnp.int32, (224, 128), 0)
    acc = jnp.zeros((224, 128), jnp.float32)
    for i in range(5):
        gap = 16 * (i + 1)
        keep = (row >= starts[i] + gap) & (row < starts[i + 1] + gap)
        acc = jnp.where(keep, buf[80 - gap : 304 - gap, :], acc)
    out[0:224, :] = acc


def fill_taps(spread_rows, wide, taps, b, shift):
    wide[0:224, :] = jnp.where(left((224, 128)), spread_rows[0:224, :], spread_rows[1:225, :])
    for p in range(8):
        off = 2 * p + shift
        taps[ROWS * b : ROWS * b + ROWS, 128 * p : 128 * p + 128] = low(wide[off : off + ROWS, :])


def fill_regions(starts, reg):
    row = lax.broadcasted_iota(jnp.int32, (336, 128), 0) - 64
    region = jnp.zeros((336, 128), jnp.int32)
    for i in range(1, 5):
        region = region + (row >= starts[i] + 16 * i).astype(jnp.int32)
    reg[...] = jnp.where((row >= 0) & (row < ROWS), region, -1)


def merge(y, b, reg, total, outs, starts):
    lo = left((224, 128))
    mine = jnp.where(lo, reg[64:288, :], reg[48:272, :])
    acc = jnp.zeros((224, 128), jnp.float32)
    for m in range(4):
        first = ROWS * b + 32 * m
        acc = acc + jnp.where(reg[32 * m : 32 * m + 224, :] == mine, y[first : first + 224, 128 * m : 128 * m + 128], 0.0)
    total[...] = acc
    part = total[0:ROWS, :] + turn(total[16 : ROWS + 16, :])
    outs[0:ROWS, :] = jnp.where(left((ROWS, 128)), part, turn(part))
    lo = left((64, 128))
    slot = lax.broadcasted_iota(jnp.int32, (64, 128), 0) + jnp.where(lo, 0, 64)
    packed = jnp.zeros((64, 128), jnp.float32)
    for i in range(5):
        gap = 16 * (i + 1)
        keep = (slot >= starts[i]) & (slot < starts[i + 1])
        packed = jnp.where(keep, jnp.where(lo, outs[gap : gap + 64, :], outs[gap + 64 : gap + 128, :]), packed)
    return low(packed)


def conv_body(lens_ref, src_ref, w, out_ref, scratch, shift):
    bufs, rows, wides, taps, regs, y, totals, outs = scratch
    blocks = [starts_of(lens_ref, pl.program_id(0) * NB + b) for b in range(NB)]
    for g in range(NB // GROUP):
        for b in range(GROUP * g, GROUP * g + GROUP):
            k = b % 2
            spread(src_ref[b, 0:64, :], blocks[b], bufs.at[k], rows.at[k])
            fill_taps(rows.at[k], wides.at[k], taps, b, shift)
        part = slice(ROWS * GROUP * g, ROWS * GROUP * (g + 1))
        y[64 + part.start : 64 + part.stop, :] = dot_nt(taps[part, :], w[...])
        if g > 0:
            merge_group(g - 1, blocks, y, regs, totals, outs, out_ref)
    merge_group(NB // GROUP - 1, blocks, y, regs, totals, outs, out_ref)


def merge_group(g, blocks, y, regs, totals, outs, out_ref):
    for b in range(GROUP * g, GROUP * g + GROUP):
        k = b % 2
        fill_regions(blocks[b], regs.at[k])
        out_ref[b] = merge(y, b, regs.at[k], totals.at[k], outs.at[k], blocks[b])


def conv_fwd_kernel(lens_ref, meta_ref, src_ref, own_ref, other_ref, out_ref, w, *scratch):
    @pl.when(pl.program_id(0) == 0)
    def _():
        x = meta_ref[2]
        for m in range(8):
            cols = slice(1024 * m, 1024 * m + 1024)
            w[pl.ds(pl.multiple_of(64 * m + 32 * x, 32), 32), :] = own_ref[:, cols]
            w[pl.ds(pl.multiple_of(64 * m + 32 * (1 - x), 32), 32), :] = other_ref[:, cols]

    conv_body(lens_ref, src_ref, w, out_ref, scratch, 0)


def conv_back_kernel(lens_ref, meta_ref, src_ref, own_ref, other_ref, out_ref, w, *scratch):
    @pl.when(pl.program_id(0) == 0)
    def _():
        x = meta_ref[2]
        for t in range(64):
            cols = slice(128 * t, 128 * t + 128)
            a, b = f32(own_ref[:, cols]), f32(other_ref[:, cols])
            pair = jnp.concatenate([jnp.where(x == 0, a, b), jnp.where(x == 0, b, a)], axis=0).T
            place = 127 - (2 * t + 1)
            m, j = place // 16, place % 16
            w[64 * m : 64 * m + 64, 64 * j : 64 * j + 64] = low(pair[64:128])
            w[64 * m : 64 * m + 64, 64 * j + 64 : 64 * j + 128] = low(pair[0:64])

    conv_body(lens_ref, src_ref, w, out_ref, scratch, 1)


def conv_grad_kernel(lens_ref, meta_ref, src_ref, g_ref, keep_ref, send_ref, acc, gt, buf, rows, wide, taps, reg, pair, regs):
    step = pl.program_id(0)
    for b in range(NB):
        starts = starts_of(lens_ref, step * NB + b)
        spread(src_ref[b, 0:64, :], starts, buf, rows)
        fill_taps(rows, wide, taps, b, 0)
        fill_regions(starts, reg)
        spread(g_ref[b, 0:64, :], starts, buf, rows.at[64:288])
        lo = left((320, 128))
        pair[16:336, :] = jnp.where(lo, rows[16:336, :], rows[0:320, :])
        regs[16:336, :] = jnp.where(lo, reg[16:336, :], reg[0:320, :])
        mine = reg[64 : 64 + ROWS, :]
        for m in range(4):
            first = 128 - 32 * m
            keep = regs[first : first + ROWS, :] == mine
            gt[ROWS * b : ROWS * b + ROWS, 128 * m : 128 * m + 128] = low(jnp.where(keep, pair[first : first + ROWS, :], 0.0))
    term = dot_tn(gt[...], taps[...])

    @pl.when(step == 0)
    def _():
        acc[...] = term

    @pl.when(step > 0)
    def _():
        acc[...] += term

    @pl.when(step == pl.num_programs(0) - 1)
    def _():
        x = meta_ref[2]
        for m in range(8):
            cols = slice(1024 * m, 1024 * m + 1024)
            keep_ref[:, cols] = acc[pl.ds(pl.multiple_of(64 * m + 32 * x, 32), 32), :]
            send_ref[:, cols] = low(acc[pl.ds(pl.multiple_of(64 * m + 32 * (1 - x), 32), 32), :])


def conv_call(kernel, lens, meta, arrays, outs, out_specs, scratch, after=(), cost=30):
    blocks = arrays[0].shape[0]
    in_specs = [
        pl.BlockSpec((NB, *a.shape[1:]), lambda i, l, m: (i, 0, 0)) if a.ndim == 3 else pl.BlockSpec(a.shape, lambda i, l, m: (0, 0))
        for a in arrays
    ]
    count = 2 + len(arrays)

    def body(*refs):
        kernel(*refs[:count], *refs[count + len(after) :])

    return pl.pallas_call(
        body,
        grid_spec=pltpu.PrefetchScalarGridSpec(
            num_scalar_prefetch=2, grid=(blocks // NB,), in_specs=in_specs + [ANY] * len(after), out_specs=out_specs, scratch_shapes=scratch
        ),
        out_shape=outs,
        compiler_params=pltpu.CompilerParams(vmem_limit_bytes=20 << 20),
        cost_estimate=estimate(cost),
    )(lens, meta, *[a if a.ndim == 3 else in_hbm(a) for a in arrays], *after)


def conv_pass(kernel, lens, meta, src, own, other, after=(), cost=30):
    scratch = [
        pltpu.VMEM((512, 1024), BF), pltpu.VMEM((2, 304, 128), F32), pltpu.VMEM((2, 232, 128), F32), pltpu.VMEM((2, 224, 128), F32),
        pltpu.VMEM((ROWS * NB, 1024), BF), pltpu.VMEM((2, 336, 128), jnp.int32), pltpu.VMEM((128 + ROWS * NB, 512), F32),
        pltpu.VMEM((2, 224, 128), F32), pltpu.VMEM((2, ROWS, 128), F32),
    ]
    spec = pl.BlockSpec((NB, 64, 128), lambda i, l, m: (i, 0, 0))
    return conv_call(kernel, lens, meta, (src, own, other), shape((src.shape[0], 64, 128)), spec, scratch, after, cost)


def conv_grads(lens, meta, src, grad, after=(), cost=30):
    scratch = [
        pltpu.VMEM((512, 1024), F32), pltpu.VMEM((ROWS * NB, 512), BF), pltpu.VMEM((304, 128), F32), pltpu.VMEM((336, 128), F32),
        pltpu.VMEM((224, 128), F32), pltpu.VMEM((ROWS * NB, 1024), BF), pltpu.VMEM((336, 128), jnp.int32), pltpu.VMEM((336, 128), F32),
        pltpu.VMEM((336, 128), jnp.int32),
    ]
    spec = pl.BlockSpec((32, 8192), lambda i, l, m: (0, 0))
    return conv_call(conv_grad_kernel, lens, meta, (src, grad), [out_hbm(shape((32, 8192), F32)), out_hbm(shape((32, 8192)))], [spec, spec], scratch, after, cost)


INV_SQRT2 = 0.7071067811865476
INV_SQRT_2PI = 0.3989422804014327


def gelu_cdf(v):
    return 0.5 + 0.5 * lax.erf(v * INV_SQRT2)


def gelu_slope(v, cdf):
    return cdf + v * (jnp.exp(-0.5 * v * v) * INV_SQRT_2PI)


def normed(v):
    centred = v - jnp.mean(v, axis=-1, keepdims=True)
    scale = lax.rsqrt(jnp.mean(centred * centred, axis=-1, keepdims=True) + norm_eps)
    return centred * scale, scale


def norm_pull(unit, scale, gain, grad):
    grad_unit = grad * gain
    mean_grad = jnp.mean(grad_unit, axis=-1, keepdims=True)
    mean_both = jnp.mean(grad_unit * unit, axis=-1, keepdims=True)
    return scale * (grad_unit - mean_grad - unit * mean_both)


def column_sum(v):
    return jnp.sum(v, axis=0, keepdims=True)


def norm_one_kernel(c_ref, f_ref, vec_ref, act_ref, zero_ref, zero_out_ref, n_ref):
    for g in range(8):
        tile = slice(128 * g, 128 * g + 128)
        a, b = cross(f32(c_ref[2 * g]), f32(c_ref[2 * g + 1]))
        act_ref[0:64, tile] = a + vec_ref[0:1, tile]
        act_ref[64:128, tile] = b + vec_ref[0:1, tile]
    for i in range(4):
        rows = slice(32 * i, 32 * i + 32)
        act = act_ref[rows, :]
        zero = f32(f_ref[rows, :]) + act * gelu_cdf(act)
        zero_ref[rows, :] = zero
        zero_out_ref[rows, :] = zero
        n_ref[rows, :] = low(normed(zero)[0] * vec_ref[1:2, :] + vec_ref[2:3, :])


def norm_two_kernel(zero_ref, keep_ref, got_ref, vec_ref, one_ref, n_ref):
    for i in range(4):
        rows = slice(32 * i, 32 * i + 32)
        one = zero_ref[rows, :] + vec_ref[5:6, :] + keep_ref[rows, :] + f32(got_ref[rows, :])
        one_ref[rows, :] = one
        n_ref[rows, :] = low(normed(one)[0] * vec_ref[6:7, :] + vec_ref[7:8, :])


def norm_two_back_kernel(keep_ref, got_ref, got_y_ref, got_d_ref, one_ref, g_ref, vec_ref, grad_ref, low_ref, sum_ref):
    sums = [jnp.zeros((1, 1024), jnp.float32) for _ in range(4)]
    for i in range(4):
        rows = slice(32 * i, 32 * i + 32)
        grad = keep_ref[rows, :] + f32(got_ref[rows, :]) + f32(got_y_ref[rows, :]) + f32(got_d_ref[rows, :])
        unit, scale = normed(one_ref[rows, :])
        out = f32(g_ref[rows, :])
        total = out + norm_pull(unit, scale, vec_ref[6:7, :], grad)
        grad_ref[rows, :] = total
        low_ref[rows, :] = low(total)
        for k, v in enumerate((total, grad * unit, grad, out)):
            sums[k] = sums[k] + column_sum(v)
    for k in range(4):
        sum_ref[k : k + 1, :] = sums[k]


def norm_one_back_kernel(meta_ref, keep_ref, got_ref, zero_ref, act_ref, one_grad_ref, vec_ref, two_ref, qv_ref, up_ref, grad_ref, pack_ref, conv):
    c, x = meta_ref[3], meta_ref[2]
    sums = [jnp.zeros((1, 1024), jnp.float32) for _ in range(3)]
    for i in range(4):
        rows = slice(32 * i, 32 * i + 32)
        grad = keep_ref[rows, :] + f32(got_ref[rows, :])
        unit, scale = normed(zero_ref[rows, :])
        total = one_grad_ref[rows, :] + norm_pull(unit, scale, vec_ref[1:2, :], grad)
        grad_ref[rows, :] = total
        act = act_ref[rows, :]
        conv_grad = total * gelu_slope(act, gelu_cdf(act))
        conv[rows, :] = conv_grad
        for k, v in enumerate((conv_grad, grad * unit, grad)):
            sums[k] = sums[k] + column_sum(v)
    lane = lax.broadcasted_iota(jnp.int32, (1, 128), 1)
    for g in range(8):
        tile = slice(128 * g, 128 * g + 128)
        p, q = cross(conv[0:64, tile], conv[64:128, tile])
        pack_ref[2 * g, 0:64, :] = low(p)
        pack_ref[2 * g + 1, 0:64, :] = low(q)
        source = qv_ref[0:2, 128 * (g // 2) : 128 * (g // 2) + 128]
        even = jnp.where(lane < 64, source, 0.0) if g % 2 == 0 else jnp.where(lane < 64, turn(source), 0.0)
        heads = jnp.where(c == 0, even, turn(even))
        up_rows = []
        for k in range(4):
            piece = up_ref[0:1, 128 * (g // 2) : 128 * (g // 2) + 128]
            piece = pltpu.roll(piece, (128 - 32 * k) % 128, 1) if k else piece
            piece = jnp.where(lane < 32, piece, 0.0)
            piece = jnp.where(x == 0, piece, pltpu.roll(piece, 32, 1))
            piece = jnp.where(c == 0, piece, turn(piece))
            up_rows.append(jnp.where(meta_ref[1] == g % 2, piece, 0.0))
        all_rows = [sums[0][:, tile], sums[1][:, tile], sums[2][:, tile], heads[0:1], heads[1:2], two_ref[0:1, tile],
                    two_ref[1:2, tile], two_ref[2:3, tile], two_ref[3:4, tile], *up_rows, jnp.zeros((3, 128), jnp.float32)]
        block = jnp.concatenate(all_rows, axis=0)
        pack_ref[2 * g, 64:80, :] = low(block)
        pack_ref[2 * g + 1, 64:80, :] = low(turn(block))


def final_kernel(c_ref, grad_ref, o_ref):
    for g in range(8):
        tile = slice(128 * g, 128 * g + 128)
        a, b = cross(f32(c_ref[2 * g]), f32(c_ref[2 * g + 1]))
        o_ref[0:64, tile] = grad_ref[0:64, tile] + a
        o_ref[64:128, tile] = grad_ref[64:128, tile] + b


def related(lens_ref, block):
    row = lax.broadcasted_iota(jnp.int32, (128, 128), 0)
    col = lax.broadcasted_iota(jnp.int32, (128, 128), 1)
    first = jnp.zeros((128, 128), jnp.int32)
    last = jnp.full((128, 128), 128, jnp.int32)
    e = 0
    for i in range(4):
        e = e + lens_ref[block * 4 + i]
        first = jnp.maximum(first, jnp.where(row >= e, e, 0))
        last = jnp.minimum(last, jnp.where(row < e, e, 128))
    return (col >= first) & (col < last)


def head_probs(query, key, rel, mine):
    masked_query = jnp.where(mine, query, jnp.zeros_like(query))
    scores = dot_nt(masked_query, key) * score_scale
    scores = jnp.where(rel, scores, -1000000000.0)
    top = jnp.max(scores, axis=-1, keepdims=True)
    expd = jnp.exp(scores - top)
    return expd / jnp.sum(expd, axis=-1, keepdims=True)


def attn_places(meta_ref, pieces, wqkv, wo):
    own, along_x, along_y, diag_a, diag_b = pieces
    y, x, c = meta_ref[1], meta_ref[2], meta_ref[3]
    groups = [[], [], [], []]
    every, low_z, high_z = slice(0, 4), slice(0, 2), slice(2, 4)
    for dy, dx, zs, src in (
        (0, 0, every, own), (0, 1, every, along_x), (1, 0, every, along_y), (1, 1, low_z, diag_a), (1, 1, high_z, diag_b)
    ):
        yy, xx = y ^ dy, x ^ dx
        for i in range(8):
            place = wqkv.at[i % 3, zs, yy, c ^ (i // 3), xx] if i < 6 else wo.at[i - 6, zs, yy, xx]
            groups[i % 3 if i < 6 else 3].append((src.at[:, i], place))
    return groups


def attn_scratch():
    return [pltpu.VMEM((3, 4, 2, 2, 2, 32, 512), BF), pltpu.VMEM((2, 4, 2, 2, 32, 512), BF)]


def attn_fwd_kernel(
    meta_ref, lens_ref, n_ref, n_other_ref, own, along_x, along_y, diag_a, diag_b, bias_ref,
    q_ref, k_ref, v_ref, m_ref, keep_ref, send_ref, wqkv, wo, ready,
):
    n = jnp.concatenate([n_ref[...], n_other_ref[...]], axis=0)
    ready(0)
    q_ref[...] = low(dot(n, wqkv[0].reshape(1024, 512)) + bias_ref[0:1, :])
    ready(1)
    k_ref[...] = low(dot(n, wqkv[1].reshape(1024, 512)))
    ready(2)
    v_ref[...] = low(dot(n, wqkv[2].reshape(1024, 512)) + bias_ref[1:2, :])
    half = lax.broadcasted_iota(jnp.int32, (128, 128), 1) // 64
    for b in range(2):
        rel = related(lens_ref, meta_ref[0] ^ b)
        for p in range(4):
            at = (slice(128 * b, 128 * b + 128), slice(128 * p, 128 * p + 128))
            query, key, value = q_ref[at], k_ref[at], v_ref[at]
            outs = [dot(low(head_probs(query, key, rel, half == h)), value) for h in range(2)]
            m_ref[at] = low(jnp.where(half == 0, outs[0], outs[1]))
    mixed = m_ref[...]
    ready(3)
    for h in range(2):
        out = dot(mixed, wo[h].reshape(512, 512))
        keep_ref[:, 512 * h : 512 * h + 512] = out[0:128]
        send_ref[:, 512 * h : 512 * h + 512] = low(out[128:256])


def attn_bwd_kernel(
    meta_ref, lens_ref, g_ref, g_other_ref, q_ref, k_ref, v_ref, own, along_x, along_y, diag_a, diag_b,
    dq_ref, dk_ref, dv_ref, sum_ref, keep_ref, send_ref, wqkv, wo, ready,
):
    grad_in = jnp.concatenate([g_ref[...], g_other_ref[...]], axis=0)
    ready(3)
    mixed_grad = low(dot_nt(grad_in[:, 0:512], wo[0].reshape(512, 512)) + dot_nt(grad_in[:, 512:1024], wo[1].reshape(512, 512)))
    half = lax.broadcasted_iota(jnp.int32, (128, 128), 1) // 64
    for p in range(4):
        sums = []
        for b in range(2):
            rel = related(lens_ref, meta_ref[0] ^ b)
            at = (slice(128 * b, 128 * b + 128), slice(128 * p, 128 * p + 128))
            query, key, value = q_ref[at], k_ref[at], v_ref[at]
            grad = mixed_grad[128 * b : 128 * b + 128, 128 * p : 128 * p + 128]
            dqs, dks, dvs = [], [], []
            for h in range(2):
                probs = head_probs(query, key, rel, half == h)
                grad_h = jnp.where(half == h, grad, jnp.zeros_like(grad))
                prob_grad = dot_nt(grad_h, value)
                dvs.append(dot_tn(low(probs), grad))
                score_grad = probs * (prob_grad - jnp.sum(probs * prob_grad, axis=-1, keepdims=True))
                score_low = low(score_grad)
                dqs.append(dot(score_low, key) * score_scale)
                dks.append(dot_tn(score_low, query) * score_scale)
            dq = jnp.where(half == 0, dqs[0], dqs[1])
            dk = jnp.where(half == 0, dks[0], dks[1])
            dv = jnp.where(half == 0, dvs[0], dvs[1])
            dq_ref[at], dk_ref[at], dv_ref[at] = low(dq), low(dk), low(dv)
            sums.append((column_sum(dq), column_sum(dv)))
        sum_ref[0:1, 128 * p : 128 * p + 128] = sums[0][0] + sums[1][0]
        sum_ref[1:2, 128 * p : 128 * p + 128] = sums[0][1] + sums[1][1]
    for j in range(3):
        ready(j)
    out = dot_nt(dq_ref[...], wqkv[0].reshape(1024, 512))
    out += dot_nt(dk_ref[...], wqkv[1].reshape(1024, 512))
    out += dot_nt(dv_ref[...], wqkv[2].reshape(1024, 512))
    keep_ref[...] = out[0:128]
    send_ref[...] = low(out[128:256])


def term_plan(meta_ref, own, send_x, send_y, keep_a, keep_b, gqkv, go):
    y, x, c = meta_ref[1], meta_ref[2], meta_ref[3]
    plan = []
    for dy, dx in ((0, 0), (0, 1), (1, 0), (1, 1)):
        yy, xx = y ^ dy, x ^ dx
        for i in range(8):
            if dy == 0 and dx == 0:
                part = own.at[:, i]
            elif i < 4:
                part = send_x.at[dy, :, i] if dx == 1 else keep_a.at[:, i]
            else:
                part = send_y.at[dx, :, i - 4] if dy == 1 else keep_b.at[:, i - 4]
            plan.append((gqkv.at[i % 3, :, yy, c ^ (i // 3), xx] if i < 6 else go.at[i - 6, :, yy, xx], part))
    return plan


def attn_term_kernel(meta_ref, n_ref, n_other_ref, dq_ref, dk_ref, dv_ref, m_ref, g_ref, g_other_ref, own, send_x, send_y, keep_a, keep_b, gqkv, go, sems):
    for z in range(4):
        cols = slice(256 * z, 256 * z + 256)
        n = jnp.concatenate([n_ref[:, cols], n_other_ref[:, cols]], axis=0)
        for j, ref in enumerate((dq_ref, dk_ref, dv_ref)):
            gqkv[j, z] = low(dot_tn(n, ref[...])).reshape(2, 2, 2, 32, 512)
    grad = jnp.concatenate([g_ref[...], g_other_ref[...]], axis=0)
    for z in range(4):
        term = low(dot_tn(m_ref[:, 128 * z : 128 * z + 128], grad))
        for h in range(2):
            go[h, z] = term[:, 512 * h : 512 * h + 512].reshape(2, 2, 32, 512)
    run_copies(term_plan(meta_ref, own, send_x, send_y, keep_a, keep_b, gqkv, go), sems)


def ffn_plan(both, wu, wd):
    return [[(both.at[:, 0:256], wu)], [(both.at[:, 256:384], wd.at[0]), (both.at[:, 384:512], wd.at[1])]]


def ffn_scratch():
    return [pltpu.VMEM((4, 256, 512), BF), pltpu.VMEM((2, 4, 128, 512), BF)]


def ffn_kernel(*refs):
    n_refs, g_refs, bias_ref = refs[0:8], refs[8:16], refs[17]
    act_ref, ug_ref, keep_ref, send_ref, sum_ref, wu, wd, ready = refs[18:26]
    ready(0)
    total = jnp.zeros((1, 512), jnp.float32)
    for i in (4, 5, 6, 7, 0, 1, 2, 3):
        rows = slice(128 * i, 128 * i + 128)
        up_pre = dot(n_refs[i][...], wu[...].reshape(1024, 512)) + bias_ref[...]
        cdf = gelu_cdf(up_pre)
        act_ref[rows, :] = low(up_pre * cdf)
        if i == 4:
            ready(1)
        act_grad = dot_nt(g_refs[i][:, 0:512], wd[0].reshape(512, 512)) + dot_nt(g_refs[i][:, 512:1024], wd[1].reshape(512, 512))
        up_grad = act_grad * gelu_slope(up_pre, cdf)
        total = total + column_sum(up_grad)
        ug_ref[rows, :] = low(up_grad)
        back = dot_nt(low(up_grad), wu[...].reshape(1024, 512))
        if i >= 4:
            send_ref[128 * i - 512 : 128 * i - 384, :] = low(back)
        else:
            keep_ref[rows, :] = back
    sum_ref[...] = total


def ffn_out_kernel(act_ref, both_ref, keep_ref, send_ref, wd, ready):
    ready(0)
    for h in range(2):
        cols = slice(512 * h, 512 * h + 512)
        keep_ref[:, cols] = dot(act_ref[0:512, :], wd[h].reshape(512, 512))
        send_ref[:, cols] = low(dot(act_ref[512:1024, :], wd[h].reshape(512, 512)))


def half_sum_kernel(keep_ref, got_ref, own_ref, x_ref, y_ref, across_ref):
    own_ref[...] = keep_ref[0:128, :] + f32(got_ref[0:128, :])
    for i, ref in enumerate((x_ref, y_ref, across_ref), 1):
        rows = slice(128 * i, 128 * i + 128)
        ref[...] = low(keep_ref[rows, :] + f32(got_ref[rows, :]))


def ffn_terms(act, grads, normeds, up_grad, after, cost=20):
    def body(*refs):
        act_ref, g_refs, n_refs, u_ref, out_ref = refs[0], refs[1:9], refs[9:17], refs[17], refs[-1]
        n = jnp.concatenate([ref[...] for ref in n_refs], axis=0)
        out_ref[0, 0:256] = low(dot_tn(n, u_ref[...]))
        g = jnp.concatenate([ref[...] for ref in g_refs], axis=0)
        down = low(dot_tn(act_ref[...], g))
        out_ref[0, 256:384] = down[:, 0:512]
        out_ref[0, 384:512] = down[:, 512:1024]

    rows = pl.BlockSpec((128, 1024), lambda i: (0, 0))
    part = pl.BlockSpec((128, 256), lambda i: (0, i))
    return pl.pallas_call(
        body,
        grid=(4,),
        in_specs=[pl.BlockSpec((1024, 128), lambda i: (0, i))] + [rows] * 8 + [part] * 8
        + [pl.BlockSpec((1024, 512), lambda i: (0, 0))] + [ANY] * len(after),
        out_specs=pl.BlockSpec((1, 512, 512), lambda i: (i, 0, 0)),
        out_shape=out_hbm(shape((4, 512, 512))),
        compiler_params=pltpu.CompilerParams(vmem_limit_bytes=20 << 20),
        cost_estimate=estimate(20),
    )(act, grads[0], *[in_hbm(v) for v in grads[1:]], normeds[0], *[in_hbm(v) for v in normeds[1:]], up_grad, *after)


def fold_call(keep_a, keep_b, got_x, got_y, after, cost=3):
    def body(a_ref, b_ref, x_ref, y_ref, *refs):
        refs[-2][...] = low(f32(a_ref[...]) + f32(x_ref[0]))
        refs[-1][...] = low(f32(b_ref[...]) + f32(y_ref[0]))

    part = pl.BlockSpec((2, 4, 32, 512), lambda i: (i, 0, 0, 0))
    second = pl.BlockSpec((1, 2, 4, 32, 512), lambda i: (1, i, 0, 0, 0))
    return pl.pallas_call(
        body,
        grid=(2,),
        in_specs=[part, part, second, second] + [ANY] * len(after),
        out_specs=[part, part],
        out_shape=[out_hbm(shape((4, 4, 32, 512)))] * 2,
        compiler_params=pltpu.CompilerParams(vmem_limit_bytes=16 << 20),
        cost_estimate=estimate(cost),
    )(in_hbm(keep_a), in_hbm(keep_b), in_hbm(got_x), in_hbm(got_y), *after)


def join_call(own, got_x, got_y, last_a, last_b, after, cost=3):
    def body(own_ref, x_ref, y_ref, a_ref, b_ref, *refs):
        refs[-1][:, 0:4] = low(f32(own_ref[:, 0:4]) + f32(x_ref[0]) + f32(a_ref[...]))
        refs[-1][:, 4:8] = low(f32(own_ref[:, 4:8]) + f32(y_ref[0]) + f32(b_ref[...]))

    full = pl.BlockSpec((2, 8, 32, 512), lambda i: (i, 0, 0, 0))
    part = pl.BlockSpec((2, 4, 32, 512), lambda i: (i, 0, 0, 0))
    first = pl.BlockSpec((1, 2, 4, 32, 512), lambda i: (0, i, 0, 0, 0))
    return pl.pallas_call(
        body,
        grid=(2,),
        in_specs=[full, first, first, part, part] + [ANY] * len(after),
        out_specs=full,
        out_shape=out_hbm(shape((4, 8, 32, 512))),
        compiler_params=pltpu.CompilerParams(vmem_limit_bytes=16 << 20),
        cost_estimate=estimate(cost),
    )(in_hbm(own), in_hbm(got_x), in_hbm(got_y), in_hbm(last_a), in_hbm(last_b), *after)


def output_kernel(one_ref, keep_ref, got_ref, got_y_ref, got_d_ref, vec_ref, o_ref):
    got = f32(got_ref[...]) + f32(got_y_ref[...]) + f32(got_d_ref[...])
    o_ref[...] = low(one_ref[...] + keep_ref[...] + got + vec_ref[8:9, :])


def up_grad_kernel(got_ref, sum_ref, up_ref, down_ref):
    for z in range(4):
        for k in range(8):
            at = 128 * (8 * z + k)
            up_ref[:, at : at + 128] = f32(got_ref[k, :, 128 * z : 128 * z + 128])
    down_ref[:, 0:512] = f32(sum_ref[256:384])
    down_ref[:, 512:1024] = f32(sum_ref[384:512])


def qkv_grad_kernel(meta_ref, sum_ref, got_ref, q_ref, k_ref, v_ref, o_ref):
    c = meta_ref[3]
    for j, ref in enumerate((q_ref, k_ref, v_ref)):
        for t in range(4):
            tile = slice(128 * t, 128 * t + 128)
            mine, theirs = f32(sum_ref[j, :, tile]), f32(got_ref[3 + j, :, tile])
            a, b = cross(jnp.where(c == 0, mine, theirs), jnp.where(c == 0, theirs, mine))
            ref[:, 256 * t : 256 * t + 128] = a
            ref[:, 256 * t + 128 : 256 * t + 256] = b
    for h in range(2):
        o_ref[:, 512 * h : 512 * h + 512] = f32(sum_ref[6 + h])


def swap(v, axis):
    return lax.ppermute(v, axis, [(0, 1), (1, 0)])


def swap_across(v):
    return lax.ppermute(v, ("y", "x"), [(i, 3 - i) for i in range(4)])


def gather_z(v):
    return lax.all_gather(v, "z", axis=0, tiled=False)


def scatter_z(v):
    return lax.psum_scatter(v, "z", scatter_dimension=0, tiled=False)


def pick(v, index, axis):
    return lax.dynamic_index_in_dim(v, index, axis, keepdims=False)


def local(
    frames, lengths, cotangent, conv_kernel, conv_bias, norm_one_gain, norm_one_bias,
    query_weight, query_bias, key_weight, value_weight, value_bias, out_weight, out_bias,
    norm_two_gain, norm_two_bias, up_weight, up_bias, down_weight, down_bias,
):
    zi, yi, ci, xi = (lax.axis_index(a) for a in ("z", "y", "c", "x"))
    meta = jnp.stack([(zi * 2 + yi) * 2 + ci, yi, xi, ci]).astype(jnp.int32)
    row, row_f, half = shape((128, 1024)), shape((128, 1024), F32), shape((256, 512))
    groups, plane = ("z", "y", "c"), ("y", "c", "x")

    def spread_plane(own, along_x, along_y, across):
        four = (own, along_x, along_y, across)
        return (*four, *(swap(v, "c") for v in four))

    def half_sum(keep, send, saved, cost, after):
        return whole_call(
            half_sum_kernel, (keep, swap(send, "c")), [saved, VMEM], [row_f, row, row, row], [saved] + [VMEM] * 3, cost=cost, after=after
        )

    vectors = (conv_bias, norm_one_gain, norm_one_bias, query_bias, value_bias, out_bias, norm_two_gain, norm_two_bias, down_bias, up_bias)
    qkv_mine, qkv_theirs, out_part, small = whole_call(
        first_kernel, (lengths, *vectors, query_weight, key_weight, value_weight, out_weight), [None] * 15,
        [shape((3, 32, 512)), shape((3, 32, 512)), shape((2, 32, 512)), shape((16, 128), F32)], [VMEM] * 4, cost=0.05, after=(),
    )
    attn_part = jnp.concatenate([qkv_mine, swap(qkv_theirs, "c"), out_part], axis=0)
    attn_own = gather_z(attn_part)

    up_split, grad_out, grad_send = whole_call(
        ffn_prep_kernel, (lengths, up_weight, cotangent), [None] * 3, [shape((8, 32, 512)), row, row], [VMEM] * 3, cost=0.05, after=(qkv_mine,)
    )
    grad_y = swap(grad_send, "y")
    up_part = lax.all_to_all(up_split, plane, 0, 0, tiled=True)

    payload = whole_call(pack_kernel, (frames, small), [None, VMEM], shape((16, 80, 128)), VMEM, cost=0.05, after=(in_hbm(attn_part), in_hbm(grad_y)))
    got = lax.all_to_all(payload, groups, 0, 0, tiled=True)
    kernel_other = swap(conv_kernel, "x")
    grad_x = swap(tie(grad_send, kernel_other), "x")
    lens = got[:, 77, 0:4].astype(jnp.int32).reshape(64)
    ffn_part = jnp.concatenate([up_part.reshape(256, 512), down_weight[:, :512], down_weight[:, 512:]], axis=0)
    ffn_both = gather_z(ffn_part)
    conv_out = conv_pass(conv_fwd_kernel, lens, meta, got, conv_kernel, kernel_other, cost=30, after=(in_hbm(attn_own), in_hbm(grad_x)))
    conv_got = lax.all_to_all(conv_out, groups, 0, 0, tiled=True)

    grad_d = swap_across(tie(grad_send, kernel_other))
    grads_out = spread_plane(grad_out, grad_x, grad_y, grad_d)
    attn_own = attn_own
    attn_x, attn_y = swap(attn_own, "x"), swap(attn_own, "y")
    diag_a, diag_b = swap(attn_x[0:2], "y"), swap(attn_y[2:4], "x")
    attn_pieces = (attn_own, attn_x, attn_y, diag_a, diag_b)

    got_small = got[:, 64:80]
    got_small_other = swap(got_small, "x")
    vec, up_bias_own, qv_bias = whole_call(
        vector_kernel, (meta, got_small, got_small_other), [SMEM, VMEM, VMEM],
        [shape((16, 1024), F32), shape((1, 512), F32), shape((2, 512), F32)], [VMEM] * 3, cost=3, after=(conv_out,),
    )
    conv_act, hidden_zero, zero_saved, n_one = whole_call(
        norm_one_kernel, (conv_got, frames, vec), [VMEM, None, VMEM], [row_f, row_f, row_f, row], [None, VMEM, None, VMEM],
        cost=1, after=(*(in_hbm(v) for v in grads_out[3:]), in_hbm(attn_x), in_hbm(attn_y)),
    )
    n_one_other = swap(n_one, "c")

    def attn_copies(first):
        return lambda *refs: attn_places(refs[0], refs[first : first + 5], refs[-2], refs[-1])

    query, key, value, mixed, attn_keep, attn_send = whole_call(
        attn_fwd_kernel, (meta, lens, n_one, n_one_other, *attn_pieces, qv_bias), [SMEM, SMEM, VMEM, VMEM] + [ANY] * 5 + [VMEM],
        [half] * 4 + [row_f, row], [None] * 4 + [VMEM] * 2, attn_scratch(), plan=attn_copies(4), vmem=16, cost=8, after=(),
    )
    hidden_one, n_two = whole_call(
        norm_two_kernel, (hidden_zero, attn_keep, swap(attn_send, "c"), vec), [VMEM] * 4, [row_f, row], [VMEM] * 2,
        cost=0.1, after=(in_hbm(ffn_both),),
    )

    n_twos = spread_plane(n_two, swap(n_two, "x"), swap(n_two, "y"), swap_across(n_two))
    many, many_f, many_half = shape((1024, 512)), shape((512, 1024), F32), shape((512, 1024))
    activated, up_grad, back_keep, back_send, up_bias_term = whole_call(
        ffn_kernel, (*n_twos, *grads_out, ffn_both, up_bias_own), ([VMEM] + [None] * 7) * 2 + [ANY, VMEM],
        [many, many, many_f, many_half, shape((1, 512), F32)], [VMEM] * 5, ffn_scratch(),
        plan=lambda *refs: ffn_plan(refs[16], refs[-2], refs[-1]), vmem=20, cost=30,
    )
    two_own, two_x, two_y, two_across = half_sum(back_keep, back_send, VMEM, 0.05, ())
    ffn_keep, ffn_send = whole_call(
        ffn_out_kernel, (activated, ffn_both), [VMEM, ANY], [many_f, many_half], [None, None], ffn_scratch()[1:],
        plan=lambda *refs: ffn_plan(refs[1], None, refs[-1])[1:], cost=1, after=(two_x,),
    )
    two_got = (swap(two_x, "x"), swap(two_y, "y"), swap_across(two_across))
    ffn_term = ffn_terms(activated, grads_out, n_twos, up_grad, (two_x,), 20)
    one_grad, attn_grad, two_sums = whole_call(
        norm_two_back_kernel, (two_own, *two_got, hidden_one, grad_out, vec), [VMEM] * 7, [row_f, row, shape((4, 1024), F32)],
        [None, VMEM, None], cost=5, after=(in_hbm(ffn_term), in_hbm(ffn_send)),
    )
    attn_grad_other = swap(attn_grad, "c")
    ffn_sum = scatter_z(ffn_term)
    dq, dk, dv, qv_sum, one_keep, one_send = whole_call(
        attn_bwd_kernel, (meta, lens, attn_grad, attn_grad_other, query, key, value, *attn_pieces),
        [SMEM, SMEM, VMEM, VMEM] + [None] * 3 + [ANY] * 5, [half] * 3 + [shape((2, 512), F32), row_f, row], [VMEM] * 6, attn_scratch(),
        plan=attn_copies(7), vmem=16, cost=70, after=(),
    )
    zero_grad, payload_back = whole_call(
        norm_one_back_kernel, (meta, one_keep, swap(one_send, "c"), zero_saved, conv_act, one_grad, vec, two_sums, qv_sum, up_bias_term),
        [SMEM, VMEM, VMEM, None, None, None, VMEM, None, VMEM, VMEM], [row_f, shape((16, 80, 128))], [None, VMEM],
        [pltpu.VMEM((128, 1024), F32)], cost=10, after=(),
    )
    grad_got = lax.all_to_all(payload_back, groups, 0, 0, tiled=True)
    out_own, out_x, out_y, out_across = half_sum(ffn_keep, ffn_send, None, 0.05, (payload_back,))

    piece, part = out_hbm(shape((4, 8, 32, 512))), out_hbm(shape((4, 4, 32, 512)))
    pair = out_hbm(shape((2, 4, 4, 32, 512)))
    term_own, term_x, term_y, keep_a, keep_b = whole_call(
        attn_term_kernel, (meta, n_one, n_one_other, dq, dk, dv, mixed, attn_grad, attn_grad_other),
        [SMEM, VMEM, VMEM] + [None] * 4 + [VMEM] * 2, [piece, pair, pair, part, part], [HBM] * 5,
        attn_scratch() + [pltpu.SemaphoreType.DMA((32,))], vmem=16, cost=1, after=(payload_back,),
    )
    got_x, got_y = swap(term_x, "x"), swap(term_y, "y")
    conv_back_out = conv_pass(conv_back_kernel, lens, meta, grad_got, conv_kernel, kernel_other, cost=10, after=(out_x,))
    send_a, send_b = fold_call(keep_a, keep_b, got_x, got_y, (conv_back_out,), 3)
    back_got = lax.all_to_all(conv_back_out, groups, 0, 0, tiled=True)
    out_got = (swap(tie(out_x, send_b), "x"), swap(tie(out_y, send_b), "y"), swap_across(tie(out_across, send_b)))
    kernel_keep, kernel_send = conv_grads(lens, meta, got, grad_got, cost=30, after=(conv_back_out,))
    last_a, last_b = swap(send_a, "y"), swap(send_b, "x")
    attn_half = join_call(term_own, got_x, got_y, last_a, last_b, (kernel_send, back_got, in_hbm(ffn_sum)), 3)
    attn_sum = scatter_z(attn_half)

    frames_grad = whole_call(final_kernel, (back_got, zero_grad), [VMEM, None], row_f, None, cost=0.05, after=(in_hbm(attn_half),))
    output = whole_call(
        output_kernel, (hidden_one, out_own, *out_got, vec), [VMEM, None] + [VMEM] * 4, row, None, cost=0.05, after=(in_hbm(attn_half),)
    )
    kernel_grad = kernel_keep + f32(swap(kernel_send, "x"))
    ffn_sum = tie(ffn_sum, attn_half)
    up_got = lax.all_to_all(ffn_sum[0:256].reshape(8, 32, 512), plane, 0, 0, tiled=True)
    up_weight_grad, down_weight_grad = whole_call(
        up_grad_kernel, (up_got, ffn_sum), [VMEM, None], [shape((32, 4096), F32), shape((128, 1024), F32)], [None] * 2, cost=0.05
    )
    small_sum = jnp.sum(f32(grad_got[:, 64:80, 0:64]), axis=0).reshape(16, 2, 32)
    small_grad = pick(small_sum, xi, 1) + swap(tie(pick(small_sum, 1 - xi, 1), send_a), "x")
    small_grads = [small_grad[i] for i in range(9)]
    attn_sum = tie(attn_sum, output, up_weight_grad, kernel_grad, small_grad, frames_grad)
    query_weight_grad, key_weight_grad, value_weight_grad, out_weight_grad = whole_call(
        qkv_grad_kernel, (meta, attn_sum, swap(attn_sum, "c")), [SMEM, None, None], [shape((32, 1024), F32)] * 4, [None] * 4
    )

    return (
        output, frames_grad, kernel_grad, small_grads[0], small_grads[1], small_grads[2], query_weight_grad, small_grads[3],
        key_weight_grad, value_weight_grad, small_grads[4], out_weight_grad, small_grads[5], small_grads[6], small_grads[7],
        up_weight_grad, small_grad[9:13].reshape(128), down_weight_grad, small_grads[8],
    )


MATRICES_IN = (0, 1, 2, 3, 7, 9, 10, 12, 16, 18)
MATRICES_OUT = (0, 1, 2, 6, 8, 9, 11, 15, 17)


def solution(mesh):
    n_dp, n_fsdp = mesh.shape["dp"], mesh.shape["fsdp"]
    if n_fsdp == 2 and n_dp == GROUPS:
        axes = ("z", "y", "c", "x")
        mesh = Mesh(mesh.devices.reshape(n_dp // 4, 2, 2, n_fsdp), axes)
        body = local
    else:
        axes = ("dp", "fsdp")
        body = local_plain
    in_specs = tuple(P(axes, None) if i in MATRICES_IN else P(axes) for i in range(20))
    out_specs = tuple(P(axes, None) if i in MATRICES_OUT else P(axes) for i in range(19))
    return jax.shard_map(body, mesh=mesh, in_specs=in_specs, out_specs=out_specs, check_vma=False)
```

profile of v0, /device:TPU:0, one launch (start us, length us, event | category | flops | bytes accessed | tf_op | source)
XLA Modules:
  0.0 275.8 jit_solution(5926020698487086334)
XLA Ops:
  13.7 2.9 %collective-permute-start.1 = (bf16[128,1024]{1,0:T(8,128)(2,1)S(1)}, bf16[128,1024]{1,0:T(8,128)(2,1)S(1)}, u32[]{:S(2)}, u32[]{:S(2)}) collective-permute-start(bf16[128,1024]{1,0:T(8,128)(2,1)S(1)} %get-tuple-element.86.refs_0_), channel_id=1, source_target_pairs={{0,4},{4,0},{1,5},{5,1},{2,6},{6,2},{3,7},{7,3},{8,12},{12,8},{9,1... | collective-permute-start | bytes 786440 | tf_op jit(solution)/shard_map/ppermute | solution.py:1159
  16.6 3.4 %all-to-all-start.2 = ((bf16[8,32,512]{2,1,0:T(8,128)(2,1)}), bf16[8,32,512]{2,1,0:T(8,128)(2,1)S(1)}, u32[]{:S(2)}, u32[]{:S(2)}) async-start(bf16[8,32,512]{2,1,0:T(8,128)(2,1)} %get-tuple-element.94), calls=%async_computation.2 | async-start | bytes 524288 | tf_op jit(solution)/shard_map/all_to_all | solution.py:1209
  26.6 7.2 %all-to-all-start = ((bf16[16,80,128]{2,1,0:T(8,128)(2,1)}), bf16[16,80,128]{2,1,0:T(8,128)(2,1)S(1)}, u32[]{:S(2)}, u32[]{:S(2)}) async-start(bf16[16,80,128]{2,1,0:T(8,128)(2,1)} %shard_map.341), calls=%async_computation | async-start | bytes 655360 | tf_op jit(solution)/shard_map/all_to_all | solution.py:1212
  34.4 2.9 %collective-permute-done.2.refs_1_.refs_4_ = bf16[32,8192]{1,0:T(8,128)(2,1)S(1)} collective-permute-done((bf16[32,8192]{1,0:T(8,128)(2,1)S(1)}, bf16[32,8192]{1,0:T(8,128)(2,1)S(1)}, u32[]{:S(2)}, u32[]{:S(2)}) %collective-permute-start.2) | collective-permute-done | bytes 524320 | tf_op jit(solution)/shard_map/ppermute | solution.py:1159
  39.3 2.6 collective-permute-start.5
  42.0 7.7 %all-to-all-done.refs_2_ = bf16[16,80,128]{2,1,0:T(8,128)(2,1)S(1)} async-done(((bf16[16,80,128]{2,1,0:T(8,128)(2,1)}), bf16[16,80,128]{2,1,0:T(8,128)(2,1)S(1)}, u32[]{:S(2)}, u32[]{:S(2)}) %all-to-all-start) | async-done | bytes 327712 | tf_op jit(solution)/shard_map/all_to_all | solution.py:1212
  51.9 10.0 %shard_map.343.refs_3_ = bf16[16,64,128]{2,1,0:T(8,128)(2,1)} custom-call(s32[64]{0:T(128)S(1)} %reshape.58.refs_0_.refs_1_, s32[4]{0:T(128)S(1)} %pad_add_fusion.refs_1_.refs_0_, bf16[16,80,128]{2,1,0:T(8,128)(2,1)S(1)} %all-to-all-done.refs_2_, bf16[32,8192]{1,0:T(8,128)(2,1)} %refs_3_.5, bf16[32,8192]{1,0:T(8,128)(2,1)} %copy-done.16, ...), custom_call_target="tpu_custom_call" | custom-call | flops 30000001024 | bytes 1024 | tf_op jit(solution)/shard_map/pallas_call | solution.py:739
  61.9 3.7 %all-to-all-start.1 = ((bf16[16,64,128]{2,1,0:T(8,128)(2,1)}), bf16[16,64,128]{2,1,0:T(8,128)(2,1)S(1)}, u32[]{:S(2)}, u32[]{:S(2)}) async-start(bf16[16,64,128]{2,1,0:T(8,128)(2,1)} %shard_map.343.refs_3_), calls=%async_computation.1 | async-start | bytes 524288 | tf_op jit(solution)/shard_map/all_to_all | solution.py:1219
  66.1 9.4 %collective-permute-done.10.refs_8_.refs_5_ = bf16[4,8,32,512]{3,2,1,0:T(8,128)(2,1)S(1)} collective-permute-done((bf16[4,8,32,512]{3,2,1,0:T(8,128)(2,1)}, bf16[4,8,32,512]{3,2,1,0:T(8,128)(2,1)S(1)}, u32[]{:S(2)}, u32[]{:S(2)}) %collective-permute-start.10) | collective-permute-done | bytes 1048608 | tf_op jit(solution)/shard_map/ppermute | solution.py:1159
  83.3 2.7 shard_map.345
  87.6 5.9 %collective-permute-done.13.refs_7_.refs_10_ = bf16[2,8,32,512]{3,2,1,0:T(8,128)(2,1)} collective-permute-done((bf16[2,8,32,512]{3,2,1,0:T(8,128)(2,1)}, bf16[2,8,32,512]{3,2,1,0:T(8,128)(2,1)}, u32[]{:S(2)}, u32[]{:S(2)}) %collective-permute-start.13) | collective-permute-done | bytes 524320 | tf_op jit(solution)/shard_map/ppermute | solution.py:1159
  94.2 9.5 %shard_map.346 = (bf16[256,512]{1,0:T(8,128)(2,1)}, bf16[256,512]{1,0:T(8,128)(2,1)}, bf16[256,512]{1,0:T(8,128)(2,1)}, bf16[256,512]{1,0:T(8,128)(2,1)}, f32[12...) custom-call(s32[4]{0:T(128)S(1)} %pad_add_fusion.refs_1_.refs_0_, s32[64]{0:T(128)S(1)} %reshape.58.refs_0_.refs_1_, ...), custom_call_target="tpu_custom_call" | custom-call | flops 8000000000 | bytes 1024 | tf_op jit(solution)/shard_map/pallas_call | solution.py:488
  109.7 5.7 %collective-permute-done.16.refs_1_.refs_10_ = bf16[128,1024]{1,0:T(8,128)(2,1)S(1)} collective-permute-done((bf16[128,1024]{1,0:T(8,128)(2,1)S(1)}, bf16[128,1024]{1,0:T(8,128)(2,1)S(1)}, u32[]{:S(2)}, u32[]{:S(2)}) %collective-permute-start.16) | collective-permute-done | bytes 262176 | tf_op jit(solution)/shard_map/ppermute | solution.py:1159
  115.9 4.7 %collective-permute-done.18.refs_3_.refs_12_ = bf16[128,1024]{1,0:T(8,128)(2,1)S(1)} collective-permute-done((bf16[128,1024]{1,0:T(8,128)(2,1)S(1)}, bf16[128,1024]{1,0:T(8,128)(2,1)S(1)}, u32[]{:S(2)}, u32[]{:S(2)}) %collective-permute-start.18) | collective-permute-done | bytes 262176 | tf_op jit(solution)/shard_map/ppermute | solution.py:1163
  122.9 10.3 %shard_map.348 = (bf16[1024,512]{1,0:T(8,128)(2,1)S(1)}, bf16[1024,512]{1,0:T(8,128)(2,1)S(1)}, f32[512,1024]{1,0:T(8,128)S(1)}, bf16[512,1024]{1,0:T(8,128)(2,1)S(1)}, f32[1,512]{1,0:T(1,128)S(1)}) custom-call(bf16[128,1024]{1,0:T(8,128)(2,1)S(1)} %get-tuple-element.96.refs_0_.refs_9_, bf16[128,1024]{1,0:T(8,128)(2,1)} %copy-done.27, ...), custom_call_target="tpu_custom_call" | custom-call | flops 30000001024 | bytes 1024 | tf_op jit(solution)/shard_map/pallas_call | solution.py:488
  140.2 6.2 %shard_map.351.refs_7_ = bf16[4,512,512]{2,1,0:T(8,128)(2,1)} custom-call(bf16[1024,512]{1,0:T(8,128)(2,1)S(1)} %get-tuple-element.98.refs_0_, bf16[128,1024]{1,0:T(8,128)(2,1)S(1)} %get-tuple-element.88.refs_8_.refs_1_.refs_5_, bf16[128,1024]{1,0:T(8,128)(2,1)} %collective-permute-done.3.refs_6_.refs_9_.refs_2_, bf16[128,1024]{1,0:T(8,128)(2,1)} %copy-done.17, ...), custom_call_target="tpu_custom_call" | custom-call | flops 20000000000 | bytes 1024 | tf_op jit(solution)/shard_map/pallas_call | solution.py:1082
  147.6 4.6 %shard_map.350 = (f32[512,1024]{1,0:T(8,128)}, bf16[512,1024]{1,0:T(8,128)(2,1)}) custom-call(bf16[1024,512]{1,0:T(8,128)(2,1)S(1)} %copy-done.8, bf16[4,512,512]{2,1,0:T(8,128)(2,1)} %bitcast.34, bf16[128,1024]{1,0:T(8,128)(2,1)S(1)} %get-tuple-element.101.refs_2_.refs_18_), custom_call_target="tpu_custom_call" | custom-call | flops 1000000000 | bytes 1024 | tf_op jit(solution)/shard_map/pallas_call | solution.py:488
  155.9 11.6 %shard_map.353 = (bf16[256,512]{1,0:T(8,128)(2,1)S(1)}, bf16[256,512]{1,0:T(8,128)(2,1)S(1)}, bf16[256,512]{1,0:T(8,128)(2,1)S(1)}, f32[2,512]{1,0:T(2,128)S(1)}...) custom-call(s32[4]{0:T(128)S(1)} %pad_add_fusion.refs_1_.refs_0_, s32[64]{0:T(128)S(1)} %reshape.58.refs_0_.refs_1_, ...), custom_call_target="tpu_custom_call" | custom-call | flops 70000001024 | bytes 1024 | tf_op jit(solution)/shard_map/pallas_call | solution.py:488
  169.1 5.0 %shard_map.354 = (f32[128,1024]{1,0:T(8,128)}, bf16[16,80,128]{2,1,0:T(8,128)(2,1)}) custom-call(s32[4]{0:T(128)S(1)} %pad_add_fusion.refs_1_.refs_0_, f32[128,1024]{1,0:T(8,128)S(1)} %get-tuple-element.112.refs_1_, bf16[128,1024]{1,0:T(8,128)(2,1)S(1)} %collective-permute-done.29.refs_2_, f32[128,1024]{1,0:T(8,128)} %get-tuple-element.114.refs_3_, ...), custom_call_target="tpu_custom_call" | custom-call | flops 10000000000 | bytes 1024 | tf_op jit(solution)/shard_map/pallas_call | solution.py:488
  174.2 4.9 %all-to-all-start.3 = ((bf16[16,80,128]{2,1,0:T(8,128)(2,1)}), bf16[16,80,128]{2,1,0:T(8,128)(2,1)S(1)}, u32[]{:S(2)}, u32[]{:S(2)}) async-start(bf16[16,80,128]{2,1,0:T(8,128)(2,1)} %get-tuple-element.120.refs_2_.refs_9_), calls=%async_computation.3 | async-start | bytes 655360 | tf_op jit(solution)/shard_map/all_to_all | solution.py:1282
  179.8 5.6 %shard_map.356 = (bf16[4,8,32,512]{3,2,1,0:T(8,128)(2,1)}, bf16[2,4,4,32,512]{4,3,2,1,0:T(8,128)(2,1)}, bf16[2,4,4,32,512]{4,3,2,1,0:T(8,128)(2,1)}, bf16[4,4,32...) custom-call(s32[4]{0:T(128)S(1)} %pad_add_fusion.refs_1_.refs_0_, bf16[128,1024]{1,0:T(8,128)(2,1)S(1)} %get-tuple-element.90.refs_2_.refs_1_, ...), custom_call_target="tpu_custom_call" | custom-call | flops 1000000000 | bytes 1024 | tf_op jit(solution)/shard_map/pallas_call | solution.py:488
  189.2 3.3 %shard_map.355 = (f32[128,1024]{1,0:T(8,128)}, bf16[128,1024]{1,0:T(8,128)(2,1)S(1)}, bf16[128,1024]{1,0:T(8,128)(2,1)S(1)}, bf16[128,1024]{1,0:T(8,128)(2,1)S(1)}) custom-call(f32[512,1024]{1,0:T(8,128)} %get-tuple-element.102.refs_0_, bf16[512,1024]{1,0:T(8,128)(2,1)S(1)} %collective-permute-done.24.refs_1_, ...), custom_call_target="tpu_custom_call" | custom-call | flops 50000000 | bytes 1024 | tf_op jit(solution)/shard_map/pallas_call | solution.py:488
  193.9 11.3 %shard_map.357.refs_0_.refs_4_ = bf16[16,64,128]{2,1,0:T(8,128)(2,1)} custom-call(s32[64]{0:T(128)S(1)} %reshape.58.refs_0_.refs_1_, s32[4]{0:T(128)S(1)} %pad_add_fusion.refs_1_.refs_0_, bf16[16,80,128]{2,1,0:T(8,128)(2,1)S(1)} %all-to-all-done.3.refs_2_.refs_3_, bf16[32,8192]{1,0:T(8,128)(2,1)} %refs_3_.5, bf16[32,8192]{1,0:T(8,128)(2,1)} %copy-done.16, ...), custom_call_target="tpu_custom_call" | custom-call | flops 10000000000 | bytes 1024 | tf_op jit(solution)/shard_map/pallas_call | solution.py:739
  205.2 4.8 %all-to-all-start.4 = ((bf16[16,64,128]{2,1,0:T(8,128)(2,1)}), bf16[16,64,128]{2,1,0:T(8,128)(2,1)S(1)}, u32[]{:S(2)}, u32[]{:S(2)}) async-start(bf16[16,64,128]{2,1,0:T(8,128)(2,1)} %shard_map.357.refs_0_.refs_4_), calls=%async_computation.4 | async-start | bytes 524288 | tf_op jit(solution)/shard_map/all_to_all | solution.py:1295
  217.8 13.3 %shard_map.362 = (f32[32,8192]{1,0:T(8,128)}, bf16[32,8192]{1,0:T(8,128)(2,1)}) custom-call(s32[64]{0:T(128)S(1)} %reshape.58.refs_0_.refs_1_, s32[4]{0:T(128)S(1)} %pad_add_fusion.refs_1_.refs_0_, bf16[16,80,128]{2,1,0:T(8,128)(2,1)S(1)} %copy-done.1, bf16[16,80,128]{2,1,0:T(8,128)(2,1)S(1)} %all-to-all-done.3.refs_2_.refs_3_, ...), custom_call_target="tpu_custom_call" | custom-call | flops 30000001024 | bytes 1024 | tf_op jit(solution)/shard_map/pallas_call | solution.py:739
  234.6 2.8 %shard_map.363.refs_6_.refs_2_.refs_1_ = bf16[4,8,32,512]{3,2,1,0:T(8,128)(2,1)} custom-call(bf16[4,8,32,512]{3,2,1,0:T(8,128)(2,1)} %get-tuple-element.134.own_ref, bf16[2,4,4,32,512]{4,3,2,1,0:T(8,128)(2,1)} %collective-permute-done.30.x_ref, bf16[2,4,4,32,512]{4,3,2,1,0:T(8,128)(2,1)} %collective-permute-done.31.y_ref, ...), custom_call_target="tpu_custom_call" | custom-call | flops 3000000000 | bytes 1024 | tf_op jit(solution)/shard_map/pallas_call | solution.py:1120
  242.2 4.1 %collective-permute-done.38 = f32[16,32]{1,0:T(8,128)S(1)} collective-permute-done((f32[16,32]{1,0:T(8,128)}, f32[16,32]{1,0:T(8,128)S(1)}, u32[]{:S(2)}, u32[]{:S(2)}) %collective-permute-start.38) | collective-permute-done | bytes 2080 | tf_op jit(solution)/shard_map/ppermute | solution.py:1159
  248.7 3.4 %all-to-all-start.5 = ((bf16[8,32,512]{2,1,0:T(8,128)(2,1)}), bf16[8,32,512]{2,1,0:T(8,128)(2,1)S(1)}, u32[]{:S(2)}, u32[]{:S(2)}) async-start(bf16[8,32,512]{2,1,0:T(8,128)(2,1)} %bitcast.14), calls=%async_computation.7 | async-start | bytes 524288 | tf_op jit(solution)/shard_map/all_to_all | solution.py:1308
  253.2 2.6 shard_map.365.refs_5_
  258.5 2.6 shard_map.368
  261.1 2.7 reduce-scatter.5.cloned.1.call-done
  266.3 3.0 %shard_map.370 = (f32[32,1024]{1,0:T(8,128)}, f32[32,1024]{1,0:T(8,128)}, f32[32,1024]{1,0:T(8,128)}, f32[32,1024]{1,0:T(8,128)}) custom-call(s32[4]{0:T(128)S(1)} %pad_add_fusion.refs_1_.refs_0_, bf16[8,32,512]{2,1,0:T(8,128)(2,1)} %shard_map.369.refs_1_, bf16[8,32,512]{2,1,0:T(8,128)(2,1)} %copy-done.19), custom_call_target="tpu_custom_call" | custom-call | flops 50000000 | bytes 1024 | tf_op jit(solution)/shard_map/pallas_call | solution.py:488
  (192 shorter events, 81.0 us)
Async XLA Ops:
  7.2 42.6 %all-gather.5.cloned.1.call-start = ((), (), s32[]{:S(2)}) async-start(), calls=%async_computation.10 | async-start | bytes 1310720 | tf_op jit(solution)/shard_map/all_gather | solution.py:1167
  16.6 10.0 %all-to-all-start.2 = ((bf16[8,32,512]{2,1,0:T(8,128)(2,1)}), bf16[8,32,512]{2,1,0:T(8,128)(2,1)S(1)}, u32[]{:S(2)}, u32[]{:S(2)}) async-start(bf16[8,32,512]{2,1,0:T(8,128)(2,1)} %get-tuple-element.94), calls=%async_computation.2 | async-start | bytes 524288 | tf_op jit(solution)/shard_map/all_to_all | solution.py:1209
  20.1 17.2 %collective-permute-start.2 = (bf16[32,8192]{1,0:T(8,128)(2,1)S(1)}, bf16[32,8192]{1,0:T(8,128)(2,1)S(1)}, u32[]{:S(2)}, u32[]{:S(2)}) collective-permute-start(bf16[32,8192]{1,0:T(8,128)(2,1)S(1)} %copy-done.24), channel_id=1, source_target_pairs={{0,1},{1,0},{2,3},{3,2},{4,5},{5,4},{6,7},{7,6},{8,9},{9,8},{10,11... | collective-permute-start | bytes 1572872 | tf_op jit(solution)/shard_map/ppermute | solution.py:1159
  26.6 23.1 %all-to-all-start = ((bf16[16,80,128]{2,1,0:T(8,128)(2,1)}), bf16[16,80,128]{2,1,0:T(8,128)(2,1)S(1)}, u32[]{:S(2)}, u32[]{:S(2)}) async-start(bf16[16,80,128]{2,1,0:T(8,128)(2,1)} %shard_map.341), calls=%async_computation | async-start | bytes 655360 | tf_op jit(solution)/shard_map/all_to_all | solution.py:1212
  33.8 70.0 %all-gather.7.cloned.1.call-start = ((), (), s32[]{:S(2)}) async-start(), calls=%async_computation.11 | async-start | bytes 2621440 | tf_op jit(solution)/shard_map/all_gather | solution.py:1167
  33.9 45.0 %collective-permute-start.6 = (bf16[128,1024]{1,0:T(8,128)(2,1)S(1)}, bf16[128,1024]{1,0:T(8,128)(2,1)}, u32[]{:S(2)}, u32[]{:S(2)}) collective-permute-start(bf16[128,1024]{1,0:T(8,128)(2,1)S(1)} %get-tuple-element.88.refs_8_.refs_1_.refs_5_), channel_id=1, source_target_pairs={{0,2},{2,0},{1,3},{3,1},{4,6},{6,4},{5,7},{7,5},{8,10},{10,8},{9,1... | collective-permute-start | bytes 786440 | tf_op jit(solution)/shard_map/ppermute | solution.py:1159
  38.0 13.9 %collective-permute-start.3 = (bf16[128,1024]{1,0:T(8,128)(2,1)}, bf16[128,1024]{1,0:T(8,128)(2,1)}, u32[]{:S(2)}, u32[]{:S(2)}) collective-permute-start(bf16[128,1024]{1,0:T(8,128)(2,1)} %shard_map.342), channel_id=1, source_target_pairs={{0,1},{1,0},{2,3},{3,2},{4,5},{5,4},{6,7},{7,6},{8,9},{9,8},{10,11... | collective-permute-start | bytes 786440 | tf_op jit(solution)/shard_map/ppermute | solution.py:1159
  39.3 37.0 %collective-permute-start.5 = (bf16[128,1024]{1,0:T(8,128)(2,1)}, bf16[128,1024]{1,0:T(8,128)(2,1)}, u32[]{:S(2)}, u32[]{:S(2)}) collective-permute-start(bf16[128,1024]{1,0:T(8,128)(2,1)} %shard_map.342), channel_id=1, source_target_pairs={{0,5},{1,4},{4,1},{5,0},{2,7},{3,6},{6,3},{7,2},{8,13},{9,12},{12,... | collective-permute-start | bytes 786440 | tf_op jit(solution)/shard_map/ppermute | solution.py:1163
  49.9 25.5 %collective-permute-start.10 = (bf16[4,8,32,512]{3,2,1,0:T(8,128)(2,1)}, bf16[4,8,32,512]{3,2,1,0:T(8,128)(2,1)S(1)}, u32[]{:S(2)}, u32[]{:S(2)}) collective-permute-start(bf16[4,8,32,512]{3,2,1,0:T(8,128)(2,1)} %bitcast.39), channel_id=1, source_target_pairs={{0,1},{1,0},{2,3},{3,2},{4,5},{5,4},{6,7},{7,6},{8,9},{9,8},{10,11... | collective-permute-start | bytes 3145736 | tf_op jit(solution)/shard_map/ppermute | solution.py:1159
  51.6 26.3 %collective-permute-start.11 = (bf16[4,8,32,512]{3,2,1,0:T(8,128)(2,1)}, bf16[4,8,32,512]{3,2,1,0:T(8,128)(2,1)S(1)}, u32[]{:S(2)}, u32[]{:S(2)}) collective-permute-start(bf16[4,8,32,512]{3,2,1,0:T(8,128)(2,1)} %bitcast.40), channel_id=1, source_target_pairs={{0,4},{4,0},{1,5},{5,1},{2,6},{6,2},{3,7},{7,3},{8,12},{12,8},{9,1... | collective-permute-start | bytes 3145736 | tf_op jit(solution)/shard_map/ppermute | solution.py:1159
  61.9 21.4 %all-to-all-start.1 = ((bf16[16,64,128]{2,1,0:T(8,128)(2,1)}), bf16[16,64,128]{2,1,0:T(8,128)(2,1)S(1)}, u32[]{:S(2)}, u32[]{:S(2)}) async-start(bf16[16,64,128]{2,1,0:T(8,128)(2,1)} %shard_map.343.refs_3_), calls=%async_computation.1 | async-start | bytes 524288 | tf_op jit(solution)/shard_map/all_to_all | solution.py:1219
  65.6 14.3 %collective-permute-start.4 = (bf16[16,16,128]{2,1,0:T(8,128)(2,1)S(1)}, bf16[16,16,128]{2,1,0:T(8,128)(2,1)S(1)}, u32[]{:S(2)}, u32[]{:S(2)}) collective-permute-start(bf16[16,16,128]{2,1,0:T(8,128)(2,1)S(1)} %slice.73.refs_1_), channel_id=1, source_target_pairs={{0,1},{1,0},{2,3},{3,2},{4,5},{5,4},{6,7},{7,6},{8,9},{9,8},{10,11... | collective-permute-start | bytes 196616 | tf_op jit(solution)/shard_map/ppermute | solution.py:1159
  78.9 14.6 %collective-permute-start.13 = (bf16[2,8,32,512]{3,2,1,0:T(8,128)(2,1)}, bf16[2,8,32,512]{3,2,1,0:T(8,128)(2,1)}, u32[]{:S(2)}, u32[]{:S(2)}) collective-permute-start(bf16[2,8,32,512]{3,2,1,0:T(8,128)(2,1)} %slice.74), channel_id=1, source_target_pairs={{0,4},{4,0},{1,5},{5,1},{2,6},{6,2},{3,7},{7,3},{8,12},{12,8},{9,1... | collective-permute-start | bytes 1572872 | tf_op jit(solution)/shard_map/ppermute | solution.py:1159
  79.9 14.3 %collective-permute-start.14 = (bf16[2,8,32,512]{3,2,1,0:T(8,128)(2,1)}, bf16[2,8,32,512]{3,2,1,0:T(8,128)(2,1)}, u32[]{:S(2)}, u32[]{:S(2)}) collective-permute-start(bf16[2,8,32,512]{3,2,1,0:T(8,128)(2,1)} %slice.75), channel_id=1, source_target_pairs={{0,1},{1,0},{2,3},{3,2},{4,5},{5,4},{6,7},{7,6},{8,9},{9,8},{10,11... | collective-permute-start | bytes 1572872 | tf_op jit(solution)/shard_map/ppermute | solution.py:1159
  107.8 12.8 %collective-permute-start.18 = (bf16[128,1024]{1,0:T(8,128)(2,1)S(1)}, bf16[128,1024]{1,0:T(8,128)(2,1)S(1)}, u32[]{:S(2)}, u32[]{:S(2)}) collective-permute-start(bf16[128,1024]{1,0:T(8,128)(2,1)S(1)} %get-tuple-element.96.refs_0_.refs_9_), channel_id=1, source_target_pairs={{0,5},{1,4},{4,1},{5,0},{2,7},{3,6},{6,3},{7,2},{8,13},{9,12},{12,... | collective-permute-start | bytes 786440 | tf_op jit(solution)/shard_map/ppermute | solution.py:1163
  109.7 10.9 %collective-permute-start.19 = (bf16[128,1024]{1,0:T(8,128)(2,1)S(1)}, bf16[128,1024]{1,0:T(8,128)(2,1)S(1)}, u32[]{:S(2)}, u32[]{:S(2)}) collective-permute-start(bf16[128,1024]{1,0:T(8,128)(2,1)S(1)} %get-tuple-element.96.refs_0_.refs_9_), channel_id=1, source_target_pairs={{0,2},{2,0},{1,3},{3,1},{4,6},{6,4},{5,7},{7,5},{8,10},{10,8},{9,1... | collective-permute-start | bytes 786440 | tf_op jit(solution)/shard_map/ppermute | solution.py:1159
  136.7 15.6 %collective-permute-start.25 = (bf16[128,1024]{1,0:T(8,128)(2,1)S(1)}, bf16[128,1024]{1,0:T(8,128)(2,1)S(1)}, u32[]{:S(2)}, u32[]{:S(2)}) collective-permute-start(bf16[128,1024]{1,0:T(8,128)(2,1)S(1)} %get-tuple-element.101.refs_2_.refs_18_), channel_id=1, source_target_pairs={{0,1},{1,0},{2,3},{3,2},{4,5},{5,4},{6,7},{7,6},{8,9},{9,8},{10,11... | collective-permute-start | bytes 786440 | tf_op jit(solution)/shard_map/ppermute | solution.py:1159
  138.4 13.8 %collective-permute-start.26 = (bf16[128,1024]{1,0:T(8,128)(2,1)S(1)}, bf16[128,1024]{1,0:T(8,128)(2,1)S(1)}, u32[]{:S(2)}, u32[]{:S(2)}) collective-permute-start(bf16[128,1024]{1,0:T(8,128)(2,1)S(1)} %get-tuple-element.105), channel_id=1, source_target_pairs={{0,4},{4,0},{1,5},{5,1},{2,6},{6,2},{3,7},{7,3},{8,12},{12,8},{9,1... | collective-permute-start | bytes 786440 | tf_op jit(solution)/shard_map/ppermute | solution.py:1159
  139.4 12.8 %collective-permute-start.27 = (bf16[128,1024]{1,0:T(8,128)(2,1)S(1)}, bf16[128,1024]{1,0:T(8,128)(2,1)S(1)}, u32[]{:S(2)}, u32[]{:S(2)}) collective-permute-start(bf16[128,1024]{1,0:T(8,128)(2,1)S(1)} %get-tuple-element.106), channel_id=1, source_target_pairs={{0,5},{1,4},{4,1},{5,0},{2,7},{3,6},{6,3},{7,2},{8,13},{9,12},{12,... | collective-permute-start | bytes 786440 | tf_op jit(solution)/shard_map/ppermute | solution.py:1163
  167.7 21.5 %collective-permute-start.24 = (bf16[512,1024]{1,0:T(8,128)(2,1)}, bf16[512,1024]{1,0:T(8,128)(2,1)S(1)}, u32[]{:S(2)}, u32[]{:S(2)}) collective-permute-start(bf16[512,1024]{1,0:T(8,128)(2,1)} %get-tuple-element.103.refs_8_), channel_id=1, source_target_pairs={{0,2},{2,0},{1,3},{3,1},{4,6},{6,4},{5,7},{7,5},{8,10},{10,8},{9,1... | collective-permute-start | bytes 3145736 | tf_op jit(solution)/shard_map/ppermute | solution.py:1159
  174.2 19.8 %all-to-all-start.3 = ((bf16[16,80,128]{2,1,0:T(8,128)(2,1)}), bf16[16,80,128]{2,1,0:T(8,128)(2,1)S(1)}, u32[]{:S(2)}, u32[]{:S(2)}) async-start(bf16[16,80,128]{2,1,0:T(8,128)(2,1)} %get-tuple-element.120.refs_2_.refs_9_), calls=%async_computation.3 | async-start | bytes 655360 | tf_op jit(solution)/shard_map/all_to_all | solution.py:1282
  179.0 53.6 %reduce-scatter.3.cloned.1.call-start = ((), (), s32[]{:S(2)}) async-start(), calls=%async_computation.8 | async-start | bytes 2621440 | tf_op jit(solution)/shard_map/reduce_scatter | solution.py:1171
  185.4 26.0 %collective-permute-start.30 = (bf16[2,4,4,32,512]{4,3,2,1,0:T(8,128)(2,1)}, bf16[2,4,4,32,512]{4,3,2,1,0:T(8,128)(2,1)}, u32[]{:S(2)}, u32[]{:S(2)}) collective-permute-start(bf16[2,4,4,32,512]{4,3,2,1,0:T(8,128)(2,1)} %get-tuple-element.129), channel_id=1, source_target_pairs={{0,1},{1,0},{2,3},{3,2},{4,5},{5,4},{6,7},{7,6},{8,9},{9,8},{10,11... | collective-permute-start | bytes 3145736 | tf_op jit(solution)/shard_map/ppermute | solution.py:1159
  187.3 25.5 %collective-permute-start.31 = (bf16[2,4,4,32,512]{4,3,2,1,0:T(8,128)(2,1)}, bf16[2,4,4,32,512]{4,3,2,1,0:T(8,128)(2,1)}, u32[]{:S(2)}, u32[]{:S(2)}) collective-permute-start(bf16[2,4,4,32,512]{4,3,2,1,0:T(8,128)(2,1)} %get-tuple-element.130), channel_id=1, source_target_pairs={{0,4},{4,0},{1,5},{5,1},{2,6},{6,2},{3,7},{7,3},{8,12},{12,8},{9,1... | collective-permute-start | bytes 3145736 | tf_op jit(solution)/shard_map/ppermute | solution.py:1159
  205.2 27.4 %all-to-all-start.4 = ((bf16[16,64,128]{2,1,0:T(8,128)(2,1)}), bf16[16,64,128]{2,1,0:T(8,128)(2,1)S(1)}, u32[]{:S(2)}, u32[]{:S(2)}) async-start(bf16[16,64,128]{2,1,0:T(8,128)(2,1)} %shard_map.357.refs_0_.refs_4_), calls=%async_computation.4 | async-start | bytes 524288 | tf_op jit(solution)/shard_map/all_to_all | solution.py:1295
  210.0 53.8 %reduce-scatter.5.cloned.1.call-start = ((), (), s32[]{:S(2)}) async-start(), calls=%async_computation.9 | async-start | bytes 1310720 | tf_op jit(solution)/shard_map/reduce_scatter | solution.py:1171
  215.2 17.4 %collective-permute-start.35 = (bf16[4,4,32,512]{3,2,1,0:T(8,128)(2,1)}, bf16[4,4,32,512]{3,2,1,0:T(8,128)(2,1)S(1)}, u32[]{:S(2)}, u32[]{:S(2)}) collective-permute-start(bf16[4,4,32,512]{3,2,1,0:T(8,128)(2,1)} %get-tuple-element.135.refs_1_), channel_id=1, source_target_pairs={{0,4},{4,0},{1,5},{5,1},{2,6},{6,2},{3,7},{7,3},{8,12},{12,8},{9,1... | collective-permute-start | bytes 1572872 | tf_op jit(solution)/shard_map/ppermute | solution.py:1159
  217.2 15.4 %collective-permute-start.36 = (bf16[4,4,32,512]{3,2,1,0:T(8,128)(2,1)}, bf16[4,4,32,512]{3,2,1,0:T(8,128)(2,1)S(1)}, u32[]{:S(2)}, u32[]{:S(2)}) collective-permute-start(bf16[4,4,32,512]{3,2,1,0:T(8,128)(2,1)} %get-tuple-element.131.refs_1_), channel_id=1, source_target_pairs={{0,1},{1,0},{2,3},{3,2},{4,5},{5,4},{6,7},{7,6},{8,9},{9,8},{10,11... | collective-permute-start | bytes 1572872 | tf_op jit(solution)/shard_map/ppermute | solution.py:1159
  231.1 20.9 %collective-permute-start.37 = (bf16[32,8192]{1,0:T(8,128)(2,1)}, bf16[32,8192]{1,0:T(8,128)(2,1)S(1)}, u32[]{:S(2)}, u32[]{:S(2)}) collective-permute-start(bf16[32,8192]{1,0:T(8,128)(2,1)} %get-tuple-element.136.refs_0_), channel_id=1, source_target_pairs={{0,1},{1,0},{2,3},{3,2},{4,5},{5,4},{6,7},{7,6},{8,9},{9,8},{10,11... | collective-permute-start | bytes 1572872 | tf_op jit(solution)/shard_map/ppermute | solution.py:1159
  238.8 17.0 %collective-permute-start.34 = (bf16[128,1024]{1,0:T(8,128)(2,1)}, bf16[128,1024]{1,0:T(8,128)(2,1)S(1)}, u32[]{:S(2)}, u32[]{:S(2)}) collective-permute-start(bf16[128,1024]{1,0:T(8,128)(2,1)} %shard_map.361), channel_id=1, source_target_pairs={{0,5},{1,4},{4,1},{5,0},{2,7},{3,6},{6,3},{7,2},{8,13},{9,12},{12,... | collective-permute-start | bytes 786440 | tf_op jit(solution)/shard_map/ppermute | solution.py:1163
  239.7 16.0 %collective-permute-start.33 = (bf16[128,1024]{1,0:T(8,128)(2,1)}, bf16[128,1024]{1,0:T(8,128)(2,1)S(1)}, u32[]{:S(2)}, u32[]{:S(2)}) collective-permute-start(bf16[128,1024]{1,0:T(8,128)(2,1)} %shard_map.360), channel_id=1, source_target_pairs={{0,4},{4,0},{1,5},{5,1},{2,6},{6,2},{3,7},{7,3},{8,12},{12,8},{9,1... | collective-permute-start | bytes 786440 | tf_op jit(solution)/shard_map/ppermute | solution.py:1159
  241.6 14.1 %collective-permute-start.32 = (bf16[128,1024]{1,0:T(8,128)(2,1)}, bf16[128,1024]{1,0:T(8,128)(2,1)S(1)}, u32[]{:S(2)}, u32[]{:S(2)}) collective-permute-start(bf16[128,1024]{1,0:T(8,128)(2,1)} %shard_map.359), channel_id=1, source_target_pairs={{0,1},{1,0},{2,3},{3,2},{4,5},{5,4},{6,7},{7,6},{8,9},{9,8},{10,11... | collective-permute-start | bytes 786440 | tf_op jit(solution)/shard_map/ppermute | solution.py:1159
  (52 other events, 292.3 us)
Sparse Core Ops, SparseCore 0:
  11.4 36.7 all-gather.4
  49.8 49.9 all-gather.6
  182.2 49.6 reduce-scatter.2
  237.5 26.2 reduce-scatter.4
where the time goes:
time: 277 us; the launch traced here: 276 us
  Pallas kernels  121 us (44%)
  waiting for transfers between devices  61.5 us (22%)
  starting transfers between devices  61.3 us (22%)
  local copies, waits for them, and re-layouts  15.1 us (5%)
  between operations  14.5 us (5%)
    pallas_call x19, Pallas kernels, whole_call(): pl.pallas_call(body, in_specs=[HBM if sp is None else sp for sp in in_spe...  74.8 us
    ppermute x36, waiting for transfers between devices, swap(): return lax.ppermute(v, axis, [(0, 1), (1, 0)])  45.3 us
    pallas_call x3, Pallas kernels, conv_call(): pl.pallas_call(body, grid_spec=pltpu.PrefetchScalarGridSpec(num_scalar_pr...  34.6 us
    ppermute x36, starting transfers between devices, swap(): return lax.ppermute(v, axis, [(0, 1), (1, 0)])  27.5 us
    unnamed x70, local copies, waits for them, and re-layouts  9.64 us
    all_to_all x1, waiting for transfers between devices, local(): got = lax.all_to_all(payload, groups, 0, 0, tiled=True)  7.74 us
    all_to_all x1, starting transfers between devices, local(): got = lax.all_to_all(payload, groups, 0, 0, tiled=True)  7.18 us
    ppermute x4, starting transfers between devices, swap_across(): return lax.ppermute(v, ('y', 'x'), [(i, 3 - i) for i in range(4)])  6.27 us
  transfers between devices with their start and end apart: 50, of which 23 were waited for; matrix products, arithmetic and copies ran while one was open for 3% of the time, Pallas kernels for 33%

commit v1 on v0

--- a/solution.py
+++ b/solution.py
@@ -1258,7 +1258,7 @@
     )
     two_own, two_x, two_y, two_across = half_sum(back_keep, back_send, VMEM, 0.05, ())
     ffn_keep, ffn_send = whole_call(
-        ffn_out_kernel, (activated, ffn_both), [VMEM, ANY], [many_f, many_half], [None, None], ffn_scratch()[1:],
+        ffn_out_kernel, (activated, ffn_both), [None, ANY], [many_f, many_half], [None, None], ffn_scratch()[1:],
         plan=lambda *refs: ffn_plan(refs[1], None, refs[-1])[1:], cost=1, after=(two_x,),
     )
     two_got = (swap(two_x, "x"), swap(two_y, "y"), swap_across(two_across))
@@ -1296,7 +1296,7 @@
     out_got = (swap(tie(out_x, send_b), "x"), swap(tie(out_y, send_b), "y"), swap_across(tie(out_across, send_b)))
     kernel_keep, kernel_send = conv_grads(lens, meta, got, grad_got, cost=30, after=(conv_back_out,))
     last_a, last_b = swap(send_a, "y"), swap(send_b, "x")
-    attn_half = join_call(term_own, got_x, got_y, last_a, last_b, (kernel_send, back_got, in_hbm(ffn_sum)), 3)
+    attn_half = join_call(term_own, got_x, got_y, last_a, last_b, (in_hbm(kernel_send), back_got, in_hbm(ffn_sum)), 3)
     attn_sum = scatter_z(attn_half)
 
     frames_grad = whole_call(final_kernel, (back_got, zero_grad), [VMEM, None], row_f, None, cost=0.05, after=(in_hbm(attn_half),))
@@ -1314,7 +1314,7 @@
     small_grads = [small_grad[i] for i in range(9)]
     attn_sum = tie(attn_sum, output, up_weight_grad, kernel_grad, small_grad, frames_grad)
     query_weight_grad, key_weight_grad, value_weight_grad, out_weight_grad = whole_call(
-        qkv_grad_kernel, (meta, attn_sum, swap(attn_sum, "c")), [SMEM, None, None], [shape((32, 1024), F32)] * 4, [None] * 4
+        qkv_grad_kernel, (meta, attn_sum, swap(attn_sum, "c")), [SMEM, None, VMEM], [shape((32, 1024), F32)] * 4, [None] * 4
     )
 
     return (

time: 277 us -> 275 us (level)
  local copies, waits for them, and re-layouts: 15.1 us -> 12.1 us
    unnamed x70 -> x64, local copies, waits for them, and re-layouts: 9.64 us -> 6.72 us
  transfers between devices with their start and end apart: 50 -> 50, of which waited for: 23 -> 24; matrix products, arithmetic and copies ran while one was open for 3% -> 3% of each run, Pallas kernels for 33% -> 33%
where the time goes in v1:
time: 275 us; the launch traced here: 274 us
  Pallas kernels  121 us (44%)
  waiting for transfers between devices  63.3 us (23%)
  starting transfers between devices  60.3 us (22%)
  between operations  14.5 us (5%)
  local copies, waits for them, and re-layouts  12.1 us (4%)
    pallas_call x19, Pallas kernels, whole_call(): pl.pallas_call(body, in_specs=[HBM if sp is None else sp for sp in in_spe...  74.8 us
    ppermute x36, waiting for transfers between devices, swap(): return lax.ppermute(v, axis, [(0, 1), (1, 0)])  48.1 us
    pallas_call x3, Pallas kernels, conv_call(): pl.pallas_call(body, grid_spec=pltpu.PrefetchScalarGridSpec(num_scalar_pr...  34.6 us
    ppermute x36, starting transfers between devices, swap(): return lax.ppermute(v, axis, [(0, 1), (1, 0)])  26.2 us
    all_to_all x1, waiting for transfers between devices, local(): got = lax.all_to_all(payload, groups, 0, 0, tiled=True)  7.74 us
    all_to_all x1, starting transfers between devices, local(): got = lax.all_to_all(payload, groups, 0, 0, tiled=True)  7.18 us
    unnamed x64, local copies, waits for them, and re-layouts  6.72 us
    ppermute x4, starting transfers between devices, swap_across(): return lax.ppermute(v, ('y', 'x'), [(i, 3 - i) for i in range(4)])  6.35 us
  transfers between devices with their start and end apart: 50, of which 24 were waited for; matrix products, arithmetic and copies ran while one was open for 3% of the time, Pallas kernels for 33%

profile of v1, /device:TPU:0, one launch (start us, length us, event | category | flops | bytes accessed | tf_op | source)
XLA Modules:
  0.0 273.6 jit_solution(11445974803094944781)
XLA Ops:
  13.7 2.9 %collective-permute-start.1 = (bf16[128,1024]{1,0:T(8,128)(2,1)S(1)}, bf16[128,1024]{1,0:T(8,128)(2,1)S(1)}, u32[]{:S(2)}, u32[]{:S(2)}) collective-permute-start(bf16[128,1024]{1,0:T(8,128)(2,1)S(1)} %get-tuple-element.86.refs_0_), channel_id=1, source_target_pairs={{0,4},{4,0},{1,5},{5,1},{2,6},{6,2},{3,7},{7,3},{8,12},{12,8},{9,1... | collective-permute-start | bytes 786440 | tf_op jit(solution)/shard_map/ppermute | solution.py:1159
  16.6 3.4 %all-to-all-start.2 = ((bf16[8,32,512]{2,1,0:T(8,128)(2,1)}), bf16[8,32,512]{2,1,0:T(8,128)(2,1)S(1)}, u32[]{:S(2)}, u32[]{:S(2)}) async-start(bf16[8,32,512]{2,1,0:T(8,128)(2,1)} %get-tuple-element.94), calls=%async_computation.2 | async-start | bytes 524288 | tf_op jit(solution)/shard_map/all_to_all | solution.py:1209
  26.6 7.2 %all-to-all-start = ((bf16[16,80,128]{2,1,0:T(8,128)(2,1)}), bf16[16,80,128]{2,1,0:T(8,128)(2,1)S(1)}, u32[]{:S(2)}, u32[]{:S(2)}) async-start(bf16[16,80,128]{2,1,0:T(8,128)(2,1)} %shard_map.341), calls=%async_computation | async-start | bytes 655360 | tf_op jit(solution)/shard_map/all_to_all | solution.py:1212
  34.3 2.9 %collective-permute-done.2.refs_1_.refs_4_ = bf16[32,8192]{1,0:T(8,128)(2,1)S(1)} collective-permute-done((bf16[32,8192]{1,0:T(8,128)(2,1)S(1)}, bf16[32,8192]{1,0:T(8,128)(2,1)S(1)}, u32[]{:S(2)}, u32[]{:S(2)}) %collective-permute-start.2) | collective-permute-done | bytes 524320 | tf_op jit(solution)/shard_map/ppermute | solution.py:1159
  39.3 2.6 collective-permute-start.5
  42.0 7.7 %all-to-all-done.refs_2_ = bf16[16,80,128]{2,1,0:T(8,128)(2,1)S(1)} async-done(((bf16[16,80,128]{2,1,0:T(8,128)(2,1)}), bf16[16,80,128]{2,1,0:T(8,128)(2,1)S(1)}, u32[]{:S(2)}, u32[]{:S(2)}) %all-to-all-start) | async-done | bytes 327712 | tf_op jit(solution)/shard_map/all_to_all | solution.py:1212
  51.9 10.0 %shard_map.343.refs_3_ = bf16[16,64,128]{2,1,0:T(8,128)(2,1)} custom-call(s32[64]{0:T(128)S(1)} %reshape.58.refs_0_.refs_1_, s32[4]{0:T(128)S(1)} %pad_add_fusion.refs_1_.refs_0_, bf16[16,80,128]{2,1,0:T(8,128)(2,1)S(1)} %all-to-all-done.refs_2_, bf16[32,8192]{1,0:T(8,128)(2,1)} %refs_3_.5, bf16[32,8192]{1,0:T(8,128)(2,1)} %copy-done.14, ...), custom_call_target="tpu_custom_call" | custom-call | flops 30000001024 | bytes 1024 | tf_op jit(solution)/shard_map/pallas_call | solution.py:739
  61.9 3.7 %all-to-all-start.1 = ((bf16[16,64,128]{2,1,0:T(8,128)(2,1)}), bf16[16,64,128]{2,1,0:T(8,128)(2,1)S(1)}, u32[]{:S(2)}, u32[]{:S(2)}) async-start(bf16[16,64,128]{2,1,0:T(8,128)(2,1)} %shard_map.343.refs_3_), calls=%async_computation.1 | async-start | bytes 524288 | tf_op jit(solution)/shard_map/all_to_all | solution.py:1219
  66.1 9.4 %collective-permute-done.10.refs_8_.refs_5_ = bf16[4,8,32,512]{3,2,1,0:T(8,128)(2,1)S(1)} collective-permute-done((bf16[4,8,32,512]{3,2,1,0:T(8,128)(2,1)}, bf16[4,8,32,512]{3,2,1,0:T(8,128)(2,1)S(1)}, u32[]{:S(2)}, u32[]{:S(2)}) %collective-permute-start.10) | collective-permute-done | bytes 1048608 | tf_op jit(solution)/shard_map/ppermute | solution.py:1159
  83.3 2.7 shard_map.345
  87.5 5.9 %collective-permute-done.13.refs_7_.refs_10_ = bf16[2,8,32,512]{3,2,1,0:T(8,128)(2,1)} collective-permute-done((bf16[2,8,32,512]{3,2,1,0:T(8,128)(2,1)}, bf16[2,8,32,512]{3,2,1,0:T(8,128)(2,1)}, u32[]{:S(2)}, u32[]{:S(2)}) %collective-permute-start.13) | collective-permute-done | bytes 524320 | tf_op jit(solution)/shard_map/ppermute | solution.py:1159
  94.2 9.5 %shard_map.346 = (bf16[256,512]{1,0:T(8,128)(2,1)}, bf16[256,512]{1,0:T(8,128)(2,1)}, bf16[256,512]{1,0:T(8,128)(2,1)}, bf16[256,512]{1,0:T(8,128)(2,1)}, f32[12...) custom-call(s32[4]{0:T(128)S(1)} %pad_add_fusion.refs_1_.refs_0_, s32[64]{0:T(128)S(1)} %reshape.58.refs_0_.refs_1_, ...), custom_call_target="tpu_custom_call" | custom-call | flops 8000000000 | bytes 1024 | tf_op jit(solution)/shard_map/pallas_call | solution.py:488
  109.7 5.7 %collective-permute-done.16.refs_1_.refs_10_ = bf16[128,1024]{1,0:T(8,128)(2,1)S(1)} collective-permute-done((bf16[128,1024]{1,0:T(8,128)(2,1)S(1)}, bf16[128,1024]{1,0:T(8,128)(2,1)S(1)}, u32[]{:S(2)}, u32[]{:S(2)}) %collective-permute-start.16) | collective-permute-done | bytes 262176 | tf_op jit(solution)/shard_map/ppermute | solution.py:1159
  115.9 4.7 %collective-permute-done.18.refs_3_.refs_12_ = bf16[128,1024]{1,0:T(8,128)(2,1)S(1)} collective-permute-done((bf16[128,1024]{1,0:T(8,128)(2,1)S(1)}, bf16[128,1024]{1,0:T(8,128)(2,1)S(1)}, u32[]{:S(2)}, u32[]{:S(2)}) %collective-permute-start.18) | collective-permute-done | bytes 262176 | tf_op jit(solution)/shard_map/ppermute | solution.py:1163
  122.9 10.2 %shard_map.348 = (bf16[1024,512]{1,0:T(8,128)(2,1)S(1)}, bf16[1024,512]{1,0:T(8,128)(2,1)S(1)}, f32[512,1024]{1,0:T(8,128)S(1)}, bf16[512,1024]{1,0:T(8,128)(2,1)S(1)}, f32[1,512]{1,0:T(1,128)S(1)}) custom-call(bf16[128,1024]{1,0:T(8,128)(2,1)S(1)} %get-tuple-element.96.refs_0_.refs_9_, bf16[128,1024]{1,0:T(8,128)(2,1)} %copy-done.24, ...), custom_call_target="tpu_custom_call" | custom-call | flops 30000001024 | bytes 1024 | tf_op jit(solution)/shard_map/pallas_call | solution.py:488
  140.2 6.1 %shard_map.351.refs_7_ = bf16[4,512,512]{2,1,0:T(8,128)(2,1)} custom-call(bf16[1024,512]{1,0:T(8,128)(2,1)S(1)} %get-tuple-element.98.refs_0_, bf16[128,1024]{1,0:T(8,128)(2,1)S(1)} %get-tuple-element.88.refs_8_.refs_1_.refs_5_, bf16[128,1024]{1,0:T(8,128)(2,1)} %collective-permute-done.3.refs_6_.refs_9_.refs_2_, bf16[128,1024]{1,0:T(8,128)(2,1)} %copy-done.15, ...), custom_call_target="tpu_custom_call" | custom-call | flops 20000000000 | bytes 1024 | tf_op jit(solution)/shard_map/pallas_call | solution.py:1082
  146.4 4.7 %shard_map.350 = (f32[512,1024]{1,0:T(8,128)}, bf16[512,1024]{1,0:T(8,128)(2,1)}) custom-call(bf16[1024,512]{1,0:T(8,128)(2,1)} %copy-done.6, bf16[4,512,512]{2,1,0:T(8,128)(2,1)} %bitcast.34, bf16[128,1024]{1,0:T(8,128)(2,1)S(1)} %get-tuple-element.101.refs_2_.refs_18_), custom_call_target="tpu_custom_call" | custom-call | flops 1000000000 | bytes 1024 | tf_op jit(solution)/shard_map/pallas_call | solution.py:488
  155.6 11.6 %shard_map.353 = (bf16[256,512]{1,0:T(8,128)(2,1)S(1)}, bf16[256,512]{1,0:T(8,128)(2,1)S(1)}, bf16[256,512]{1,0:T(8,128)(2,1)S(1)}, f32[2,512]{1,0:T(2,128)S(1)}...) custom-call(s32[4]{0:T(128)S(1)} %pad_add_fusion.refs_1_.refs_0_, s32[64]{0:T(128)S(1)} %reshape.58.refs_0_.refs_1_, ...), custom_call_target="tpu_custom_call" | custom-call | flops 70000001024 | bytes 1024 | tf_op jit(solution)/shard_map/pallas_call | solution.py:488
  168.9 5.0 %shard_map.354 = (f32[128,1024]{1,0:T(8,128)}, bf16[16,80,128]{2,1,0:T(8,128)(2,1)}) custom-call(s32[4]{0:T(128)S(1)} %pad_add_fusion.refs_1_.refs_0_, f32[128,1024]{1,0:T(8,128)S(1)} %get-tuple-element.112.refs_1_, bf16[128,1024]{1,0:T(8,128)(2,1)S(1)} %collective-permute-done.29.refs_2_, f32[128,1024]{1,0:T(8,128)} %get-tuple-element.114.refs_3_, ...), custom_call_target="tpu_custom_call" | custom-call | flops 10000000000 | bytes 1024 | tf_op jit(solution)/shard_map/pallas_call | solution.py:488
  174.0 5.0 %all-to-all-start.3 = ((bf16[16,80,128]{2,1,0:T(8,128)(2,1)}), bf16[16,80,128]{2,1,0:T(8,128)(2,1)S(1)}, u32[]{:S(2)}, u32[]{:S(2)}) async-start(bf16[16,80,128]{2,1,0:T(8,128)(2,1)} %get-tuple-element.120.refs_2_.refs_9_), calls=%async_computation.3 | async-start | bytes 655360 | tf_op jit(solution)/shard_map/all_to_all | solution.py:1282
  179.7 5.6 %shard_map.356 = (bf16[4,8,32,512]{3,2,1,0:T(8,128)(2,1)}, bf16[2,4,4,32,512]{4,3,2,1,0:T(8,128)(2,1)}, bf16[2,4,4,32,512]{4,3,2,1,0:T(8,128)(2,1)}, bf16[4,4,32...) custom-call(s32[4]{0:T(128)S(1)} %pad_add_fusion.refs_1_.refs_0_, bf16[128,1024]{1,0:T(8,128)(2,1)S(1)} %get-tuple-element.90.refs_2_.refs_1_, ...), custom_call_target="tpu_custom_call" | custom-call | flops 1000000000 | bytes 1024 | tf_op jit(solution)/shard_map/pallas_call | solution.py:488
  188.1 3.3 %shard_map.355 = (f32[128,1024]{1,0:T(8,128)}, bf16[128,1024]{1,0:T(8,128)(2,1)S(1)}, bf16[128,1024]{1,0:T(8,128)(2,1)S(1)}, bf16[128,1024]{1,0:T(8,128)(2,1)S(1)}) custom-call(f32[512,1024]{1,0:T(8,128)} %get-tuple-element.102.refs_0_, bf16[512,1024]{1,0:T(8,128)(2,1)S(1)} %collective-permute-done.24.refs_1_, ...), custom_call_target="tpu_custom_call" | custom-call | flops 50000000 | bytes 1024 | tf_op jit(solution)/shard_map/pallas_call | solution.py:488
  192.8 11.3 %shard_map.357.refs_0_.refs_4_ = bf16[16,64,128]{2,1,0:T(8,128)(2,1)} custom-call(s32[64]{0:T(128)S(1)} %reshape.58.refs_0_.refs_1_, s32[4]{0:T(128)S(1)} %pad_add_fusion.refs_1_.refs_0_, bf16[16,80,128]{2,1,0:T(8,128)(2,1)S(1)} %all-to-all-done.3.refs_2_.refs_3_, bf16[32,8192]{1,0:T(8,128)(2,1)} %refs_3_.5, bf16[32,8192]{1,0:T(8,128)(2,1)} %copy-done.14, ...), custom_call_target="tpu_custom_call" | custom-call | flops 10000000000 | bytes 1024 | tf_op jit(solution)/shard_map/pallas_call | solution.py:739
  204.1 4.8 %all-to-all-start.4 = ((bf16[16,64,128]{2,1,0:T(8,128)(2,1)}), bf16[16,64,128]{2,1,0:T(8,128)(2,1)S(1)}, u32[]{:S(2)}, u32[]{:S(2)}) async-start(bf16[16,64,128]{2,1,0:T(8,128)(2,1)} %shard_map.357.refs_0_.refs_4_), calls=%async_computation.4 | async-start | bytes 524288 | tf_op jit(solution)/shard_map/all_to_all | solution.py:1295
  217.4 13.3 %shard_map.362 = (f32[32,8192]{1,0:T(8,128)}, bf16[32,8192]{1,0:T(8,128)(2,1)}) custom-call(s32[64]{0:T(128)S(1)} %reshape.58.refs_0_.refs_1_, s32[4]{0:T(128)S(1)} %pad_add_fusion.refs_1_.refs_0_, bf16[16,80,128]{2,1,0:T(8,128)(2,1)S(1)} %copy-done.1, bf16[16,80,128]{2,1,0:T(8,128)(2,1)S(1)} %all-to-all-done.3.refs_2_.refs_3_, ...), custom_call_target="tpu_custom_call" | custom-call | flops 30000001024 | bytes 1024 | tf_op jit(solution)/shard_map/pallas_call | solution.py:739
  232.6 2.8 %shard_map.363.refs_6_.refs_2_.refs_1_ = bf16[4,8,32,512]{3,2,1,0:T(8,128)(2,1)} custom-call(bf16[4,8,32,512]{3,2,1,0:T(8,128)(2,1)} %get-tuple-element.134.own_ref, bf16[2,4,4,32,512]{4,3,2,1,0:T(8,128)(2,1)} %collective-permute-done.30.x_ref, bf16[2,4,4,32,512]{4,3,2,1,0:T(8,128)(2,1)} %collective-permute-done.31.y_ref, ...), custom_call_target="tpu_custom_call" | custom-call | flops 3000000000 | bytes 1024 | tf_op jit(solution)/shard_map/pallas_call | solution.py:1120
  240.8 5.1 %collective-permute-done.38 = f32[16,32]{1,0:T(8,128)S(1)} collective-permute-done((f32[16,32]{1,0:T(8,128)}, f32[16,32]{1,0:T(8,128)S(1)}, u32[]{:S(2)}, u32[]{:S(2)}) %collective-permute-start.38) | collective-permute-done | bytes 2080 | tf_op jit(solution)/shard_map/ppermute | solution.py:1159
  248.2 3.4 %all-to-all-start.5 = ((bf16[8,32,512]{2,1,0:T(8,128)(2,1)}), bf16[8,32,512]{2,1,0:T(8,128)(2,1)S(1)}, u32[]{:S(2)}, u32[]{:S(2)}) async-start(bf16[8,32,512]{2,1,0:T(8,128)(2,1)} %bitcast.14), calls=%async_computation.7 | async-start | bytes 524288 | tf_op jit(solution)/shard_map/all_to_all | solution.py:1308
  252.7 2.6 shard_map.365.refs_5_
  255.3 2.5 shard_map.364.refs_1_
  258.0 2.6 shard_map.368
  264.1 2.9 %shard_map.370 = (f32[32,1024]{1,0:T(8,128)}, f32[32,1024]{1,0:T(8,128)}, f32[32,1024]{1,0:T(8,128)}, f32[32,1024]{1,0:T(8,128)}) custom-call(s32[4]{0:T(128)S(1)} %pad_add_fusion.refs_1_.refs_0_, bf16[8,32,512]{2,1,0:T(8,128)(2,1)} %shard_map.369.refs_1_, bf16[8,32,512]{2,1,0:T(8,128)(2,1)S(1)} %collective-permute-done.39.refs_2_), custom_call_target="tpu_custom_call" | custom-call | flops 50000000 | bytes 1024 | tf_op jit(solution)/shard_map/pallas_call | solution.py:488
  (186 shorter events, 77.8 us)
Async XLA Ops:
  7.2 42.6 %all-gather.5.cloned.1.call-start = ((), (), s32[]{:S(2)}) async-start(), calls=%async_computation.10 | async-start | bytes 1310720 | tf_op jit(solution)/shard_map/all_gather | solution.py:1167
  16.6 10.0 %all-to-all-start.2 = ((bf16[8,32,512]{2,1,0:T(8,128)(2,1)}), bf16[8,32,512]{2,1,0:T(8,128)(2,1)S(1)}, u32[]{:S(2)}, u32[]{:S(2)}) async-start(bf16[8,32,512]{2,1,0:T(8,128)(2,1)} %get-tuple-element.94), calls=%async_computation.2 | async-start | bytes 524288 | tf_op jit(solution)/shard_map/all_to_all | solution.py:1209
  20.1 17.2 %collective-permute-start.2 = (bf16[32,8192]{1,0:T(8,128)(2,1)S(1)}, bf16[32,8192]{1,0:T(8,128)(2,1)S(1)}, u32[]{:S(2)}, u32[]{:S(2)}) collective-permute-start(bf16[32,8192]{1,0:T(8,128)(2,1)S(1)} %copy-done.21), channel_id=1, source_target_pairs={{0,1},{1,0},{2,3},{3,2},{4,5},{5,4},{6,7},{7,6},{8,9},{9,8},{10,11... | collective-permute-start | bytes 1572872 | tf_op jit(solution)/shard_map/ppermute | solution.py:1159
  26.6 23.1 %all-to-all-start = ((bf16[16,80,128]{2,1,0:T(8,128)(2,1)}), bf16[16,80,128]{2,1,0:T(8,128)(2,1)S(1)}, u32[]{:S(2)}, u32[]{:S(2)}) async-start(bf16[16,80,128]{2,1,0:T(8,128)(2,1)} %shard_map.341), calls=%async_computation | async-start | bytes 655360 | tf_op jit(solution)/shard_map/all_to_all | solution.py:1212
  33.8 70.0 %all-gather.7.cloned.1.call-start = ((), (), s32[]{:S(2)}) async-start(), calls=%async_computation.11 | async-start | bytes 2621440 | tf_op jit(solution)/shard_map/all_gather | solution.py:1167
  33.9 45.0 %collective-permute-start.6 = (bf16[128,1024]{1,0:T(8,128)(2,1)S(1)}, bf16[128,1024]{1,0:T(8,128)(2,1)}, u32[]{:S(2)}, u32[]{:S(2)}) collective-permute-start(bf16[128,1024]{1,0:T(8,128)(2,1)S(1)} %get-tuple-element.88.refs_8_.refs_1_.refs_5_), channel_id=1, source_target_pairs={{0,2},{2,0},{1,3},{3,1},{4,6},{6,4},{5,7},{7,5},{8,10},{10,8},{9,1... | collective-permute-start | bytes 786440 | tf_op jit(solution)/shard_map/ppermute | solution.py:1159
  38.0 13.9 %collective-permute-start.3 = (bf16[128,1024]{1,0:T(8,128)(2,1)}, bf16[128,1024]{1,0:T(8,128)(2,1)}, u32[]{:S(2)}, u32[]{:S(2)}) collective-permute-start(bf16[128,1024]{1,0:T(8,128)(2,1)} %shard_map.342), channel_id=1, source_target_pairs={{0,1},{1,0},{2,3},{3,2},{4,5},{5,4},{6,7},{7,6},{8,9},{9,8},{10,11... | collective-permute-start | bytes 786440 | tf_op jit(solution)/shard_map/ppermute | solution.py:1159
  39.3 37.0 %collective-permute-start.5 = (bf16[128,1024]{1,0:T(8,128)(2,1)}, bf16[128,1024]{1,0:T(8,128)(2,1)}, u32[]{:S(2)}, u32[]{:S(2)}) collective-permute-start(bf16[128,1024]{1,0:T(8,128)(2,1)} %shard_map.342), channel_id=1, source_target_pairs={{0,5},{1,4},{4,1},{5,0},{2,7},{3,6},{6,3},{7,2},{8,13},{9,12},{12,... | collective-permute-start | bytes 786440 | tf_op jit(solution)/shard_map/ppermute | solution.py:1163
  49.9 25.5 %collective-permute-start.10 = (bf16[4,8,32,512]{3,2,1,0:T(8,128)(2,1)}, bf16[4,8,32,512]{3,2,1,0:T(8,128)(2,1)S(1)}, u32[]{:S(2)}, u32[]{:S(2)}) collective-permute-start(bf16[4,8,32,512]{3,2,1,0:T(8,128)(2,1)} %bitcast.39), channel_id=1, source_target_pairs={{0,1},{1,0},{2,3},{3,2},{4,5},{5,4},{6,7},{7,6},{8,9},{9,8},{10,11... | collective-permute-start | bytes 3145736 | tf_op jit(solution)/shard_map/ppermute | solution.py:1159
  51.6 26.3 %collective-permute-start.11 = (bf16[4,8,32,512]{3,2,1,0:T(8,128)(2,1)}, bf16[4,8,32,512]{3,2,1,0:T(8,128)(2,1)S(1)}, u32[]{:S(2)}, u32[]{:S(2)}) collective-permute-start(bf16[4,8,32,512]{3,2,1,0:T(8,128)(2,1)} %bitcast.40), channel_id=1, source_target_pairs={{0,4},{4,0},{1,5},{5,1},{2,6},{6,2},{3,7},{7,3},{8,12},{12,8},{9,1... | collective-permute-start | bytes 3145736 | tf_op jit(solution)/shard_map/ppermute | solution.py:1159
  61.9 21.4 %all-to-all-start.1 = ((bf16[16,64,128]{2,1,0:T(8,128)(2,1)}), bf16[16,64,128]{2,1,0:T(8,128)(2,1)S(1)}, u32[]{:S(2)}, u32[]{:S(2)}) async-start(bf16[16,64,128]{2,1,0:T(8,128)(2,1)} %shard_map.343.refs_3_), calls=%async_computation.1 | async-start | bytes 524288 | tf_op jit(solution)/shard_map/all_to_all | solution.py:1219
  65.6 14.2 %collective-permute-start.4 = (bf16[16,16,128]{2,1,0:T(8,128)(2,1)S(1)}, bf16[16,16,128]{2,1,0:T(8,128)(2,1)S(1)}, u32[]{:S(2)}, u32[]{:S(2)}) collective-permute-start(bf16[16,16,128]{2,1,0:T(8,128)(2,1)S(1)} %slice.73.refs_1_), channel_id=1, source_target_pairs={{0,1},{1,0},{2,3},{3,2},{4,5},{5,4},{6,7},{7,6},{8,9},{9,8},{10,11... | collective-permute-start | bytes 196616 | tf_op jit(solution)/shard_map/ppermute | solution.py:1159
  78.9 14.6 %collective-permute-start.13 = (bf16[2,8,32,512]{3,2,1,0:T(8,128)(2,1)}, bf16[2,8,32,512]{3,2,1,0:T(8,128)(2,1)}, u32[]{:S(2)}, u32[]{:S(2)}) collective-permute-start(bf16[2,8,32,512]{3,2,1,0:T(8,128)(2,1)} %slice.74), channel_id=1, source_target_pairs={{0,4},{4,0},{1,5},{5,1},{2,6},{6,2},{3,7},{7,3},{8,12},{12,8},{9,1... | collective-permute-start | bytes 1572872 | tf_op jit(solution)/shard_map/ppermute | solution.py:1159
  79.9 14.3 %collective-permute-start.14 = (bf16[2,8,32,512]{3,2,1,0:T(8,128)(2,1)}, bf16[2,8,32,512]{3,2,1,0:T(8,128)(2,1)}, u32[]{:S(2)}, u32[]{:S(2)}) collective-permute-start(bf16[2,8,32,512]{3,2,1,0:T(8,128)(2,1)} %slice.75), channel_id=1, source_target_pairs={{0,1},{1,0},{2,3},{3,2},{4,5},{5,4},{6,7},{7,6},{8,9},{9,8},{10,11... | collective-permute-start | bytes 1572872 | tf_op jit(solution)/shard_map/ppermute | solution.py:1159
  107.8 12.8 %collective-permute-start.18 = (bf16[128,1024]{1,0:T(8,128)(2,1)S(1)}, bf16[128,1024]{1,0:T(8,128)(2,1)S(1)}, u32[]{:S(2)}, u32[]{:S(2)}) collective-permute-start(bf16[128,1024]{1,0:T(8,128)(2,1)S(1)} %get-tuple-element.96.refs_0_.refs_9_), channel_id=1, source_target_pairs={{0,5},{1,4},{4,1},{5,0},{2,7},{3,6},{6,3},{7,2},{8,13},{9,12},{12,... | collective-permute-start | bytes 786440 | tf_op jit(solution)/shard_map/ppermute | solution.py:1163
  109.7 10.9 %collective-permute-start.19 = (bf16[128,1024]{1,0:T(8,128)(2,1)S(1)}, bf16[128,1024]{1,0:T(8,128)(2,1)S(1)}, u32[]{:S(2)}, u32[]{:S(2)}) collective-permute-start(bf16[128,1024]{1,0:T(8,128)(2,1)S(1)} %get-tuple-element.96.refs_0_.refs_9_), channel_id=1, source_target_pairs={{0,2},{2,0},{1,3},{3,1},{4,6},{6,4},{5,7},{7,5},{8,10},{10,8},{9,1... | collective-permute-start | bytes 786440 | tf_op jit(solution)/shard_map/ppermute | solution.py:1159
  136.6 14.5 %collective-permute-start.25 = (bf16[128,1024]{1,0:T(8,128)(2,1)S(1)}, bf16[128,1024]{1,0:T(8,128)(2,1)S(1)}, u32[]{:S(2)}, u32[]{:S(2)}) collective-permute-start(bf16[128,1024]{1,0:T(8,128)(2,1)S(1)} %get-tuple-element.101.refs_2_.refs_18_), channel_id=1, source_target_pairs={{0,1},{1,0},{2,3},{3,2},{4,5},{5,4},{6,7},{7,6},{8,9},{9,8},{10,11... | collective-permute-start | bytes 786440 | tf_op jit(solution)/shard_map/ppermute | solution.py:1159
  138.4 13.7 %collective-permute-start.26 = (bf16[128,1024]{1,0:T(8,128)(2,1)S(1)}, bf16[128,1024]{1,0:T(8,128)(2,1)S(1)}, u32[]{:S(2)}, u32[]{:S(2)}) collective-permute-start(bf16[128,1024]{1,0:T(8,128)(2,1)S(1)} %get-tuple-element.105), channel_id=1, source_target_pairs={{0,4},{4,0},{1,5},{5,1},{2,6},{6,2},{3,7},{7,3},{8,12},{12,8},{9,1... | collective-permute-start | bytes 786440 | tf_op jit(solution)/shard_map/ppermute | solution.py:1159
  139.4 12.7 %collective-permute-start.27 = (bf16[128,1024]{1,0:T(8,128)(2,1)S(1)}, bf16[128,1024]{1,0:T(8,128)(2,1)S(1)}, u32[]{:S(2)}, u32[]{:S(2)}) collective-permute-start(bf16[128,1024]{1,0:T(8,128)(2,1)S(1)} %get-tuple-element.106), channel_id=1, source_target_pairs={{0,5},{1,4},{4,1},{5,0},{2,7},{3,6},{6,3},{7,2},{8,13},{9,12},{12,... | collective-permute-start | bytes 786440 | tf_op jit(solution)/shard_map/ppermute | solution.py:1163
  167.5 20.6 %collective-permute-start.24 = (bf16[512,1024]{1,0:T(8,128)(2,1)}, bf16[512,1024]{1,0:T(8,128)(2,1)S(1)}, u32[]{:S(2)}, u32[]{:S(2)}) collective-permute-start(bf16[512,1024]{1,0:T(8,128)(2,1)} %get-tuple-element.103.refs_8_), channel_id=1, source_target_pairs={{0,2},{2,0},{1,3},{3,1},{4,6},{6,4},{5,7},{7,5},{8,10},{10,8},{9,1... | collective-permute-start | bytes 3145736 | tf_op jit(solution)/shard_map/ppermute | solution.py:1159
  174.0 18.8 %all-to-all-start.3 = ((bf16[16,80,128]{2,1,0:T(8,128)(2,1)}), bf16[16,80,128]{2,1,0:T(8,128)(2,1)S(1)}, u32[]{:S(2)}, u32[]{:S(2)}) async-start(bf16[16,80,128]{2,1,0:T(8,128)(2,1)} %get-tuple-element.120.refs_2_.refs_9_), calls=%async_computation.3 | async-start | bytes 655360 | tf_op jit(solution)/shard_map/all_to_all | solution.py:1282
  179.0 52.6 %reduce-scatter.3.cloned.1.call-start = ((), (), s32[]{:S(2)}) async-start(), calls=%async_computation.8 | async-start | bytes 2621440 | tf_op jit(solution)/shard_map/reduce_scatter | solution.py:1171
  185.4 25.9 %collective-permute-start.30 = (bf16[2,4,4,32,512]{4,3,2,1,0:T(8,128)(2,1)}, bf16[2,4,4,32,512]{4,3,2,1,0:T(8,128)(2,1)}, u32[]{:S(2)}, u32[]{:S(2)}) collective-permute-start(bf16[2,4,4,32,512]{4,3,2,1,0:T(8,128)(2,1)} %get-tuple-element.129), channel_id=1, source_target_pairs={{0,1},{1,0},{2,3},{3,2},{4,5},{5,4},{6,7},{7,6},{8,9},{9,8},{10,11... | collective-permute-start | bytes 3145736 | tf_op jit(solution)/shard_map/ppermute | solution.py:1159
  186.1 26.3 %collective-permute-start.31 = (bf16[2,4,4,32,512]{4,3,2,1,0:T(8,128)(2,1)}, bf16[2,4,4,32,512]{4,3,2,1,0:T(8,128)(2,1)}, u32[]{:S(2)}, u32[]{:S(2)}) collective-permute-start(bf16[2,4,4,32,512]{4,3,2,1,0:T(8,128)(2,1)} %get-tuple-element.130), channel_id=1, source_target_pairs={{0,4},{4,0},{1,5},{5,1},{2,6},{6,2},{3,7},{7,3},{8,12},{12,8},{9,1... | collective-permute-start | bytes 3145736 | tf_op jit(solution)/shard_map/ppermute | solution.py:1159
  204.1 27.5 %all-to-all-start.4 = ((bf16[16,64,128]{2,1,0:T(8,128)(2,1)}), bf16[16,64,128]{2,1,0:T(8,128)(2,1)S(1)}, u32[]{:S(2)}, u32[]{:S(2)}) async-start(bf16[16,64,128]{2,1,0:T(8,128)(2,1)} %shard_map.357.refs_0_.refs_4_), calls=%async_computation.4 | async-start | bytes 524288 | tf_op jit(solution)/shard_map/all_to_all | solution.py:1295
  208.9 53.5 %reduce-scatter.5.cloned.1.call-start = ((), (), s32[]{:S(2)}) async-start(), calls=%async_computation.9 | async-start | bytes 1310720 | tf_op jit(solution)/shard_map/reduce_scatter | solution.py:1171
  215.0 16.6 %collective-permute-start.35 = (bf16[4,4,32,512]{3,2,1,0:T(8,128)(2,1)}, bf16[4,4,32,512]{3,2,1,0:T(8,128)(2,1)S(1)}, u32[]{:S(2)}, u32[]{:S(2)}) collective-permute-start(bf16[4,4,32,512]{3,2,1,0:T(8,128)(2,1)} %get-tuple-element.135.refs_1_), channel_id=1, source_target_pairs={{0,4},{4,0},{1,5},{5,1},{2,6},{6,2},{3,7},{7,3},{8,12},{12,8},{9,1... | collective-permute-start | bytes 1572872 | tf_op jit(solution)/shard_map/ppermute | solution.py:1159
  216.3 15.3 %collective-permute-start.36 = (bf16[4,4,32,512]{3,2,1,0:T(8,128)(2,1)}, bf16[4,4,32,512]{3,2,1,0:T(8,128)(2,1)S(1)}, u32[]{:S(2)}, u32[]{:S(2)}) collective-permute-start(bf16[4,4,32,512]{3,2,1,0:T(8,128)(2,1)} %get-tuple-element.131.refs_1_), channel_id=1, source_target_pairs={{0,1},{1,0},{2,3},{3,2},{4,5},{5,4},{6,7},{7,6},{8,9},{9,8},{10,11... | collective-permute-start | bytes 1572872 | tf_op jit(solution)/shard_map/ppermute | solution.py:1159
  230.7 20.9 %collective-permute-start.37 = (bf16[32,8192]{1,0:T(8,128)(2,1)}, bf16[32,8192]{1,0:T(8,128)(2,1)S(1)}, u32[]{:S(2)}, u32[]{:S(2)}) collective-permute-start(bf16[32,8192]{1,0:T(8,128)(2,1)} %get-tuple-element.136.refs_0_), channel_id=1, source_target_pairs={{0,1},{1,0},{2,3},{3,2},{4,5},{5,4},{6,7},{7,6},{8,9},{9,8},{10,11... | collective-permute-start | bytes 1572872 | tf_op jit(solution)/shard_map/ppermute | solution.py:1159
  237.3 17.9 %collective-permute-start.34 = (bf16[128,1024]{1,0:T(8,128)(2,1)}, bf16[128,1024]{1,0:T(8,128)(2,1)S(1)}, u32[]{:S(2)}, u32[]{:S(2)}) collective-permute-start(bf16[128,1024]{1,0:T(8,128)(2,1)} %shard_map.361), channel_id=1, source_target_pairs={{0,5},{1,4},{4,1},{5,0},{2,7},{3,6},{6,3},{7,2},{8,13},{9,12},{12,... | collective-permute-start | bytes 786440 | tf_op jit(solution)/shard_map/ppermute | solution.py:1163
  238.4 16.9 %collective-permute-start.33 = (bf16[128,1024]{1,0:T(8,128)(2,1)}, bf16[128,1024]{1,0:T(8,128)(2,1)S(1)}, u32[]{:S(2)}, u32[]{:S(2)}) collective-permute-start(bf16[128,1024]{1,0:T(8,128)(2,1)} %shard_map.360), channel_id=1, source_target_pairs={{0,4},{4,0},{1,5},{5,1},{2,6},{6,2},{3,7},{7,3},{8,12},{12,8},{9,1... | collective-permute-start | bytes 786440 | tf_op jit(solution)/shard_map/ppermute | solution.py:1159
  239.7 15.6 %collective-permute-start.32 = (bf16[128,1024]{1,0:T(8,128)(2,1)}, bf16[128,1024]{1,0:T(8,128)(2,1)S(1)}, u32[]{:S(2)}, u32[]{:S(2)}) collective-permute-start(bf16[128,1024]{1,0:T(8,128)(2,1)} %shard_map.359), channel_id=1, source_target_pairs={{0,1},{1,0},{2,3},{3,2},{4,5},{5,4},{6,7},{7,6},{8,9},{9,8},{10,11... | collective-permute-start | bytes 786440 | tf_op jit(solution)/shard_map/ppermute | solution.py:1159
  (49 other events, 290.6 us)
Sparse Core Ops, SparseCore 0:
  11.4 36.7 all-gather.4
  49.8 49.9 all-gather.6
  182.1 48.5 reduce-scatter.2
  235.6 26.7 reduce-scatter.4

commit v2 on v1

--- a/solution.py
+++ b/solution.py
@@ -1007,17 +1007,28 @@
 
 
 def attn_term_kernel(meta_ref, n_ref, n_other_ref, dq_ref, dk_ref, dv_ref, m_ref, g_ref, g_other_ref, own, send_x, send_y, keep_a, keep_b, gqkv, go, sems):
-    for z in range(4):
-        cols = slice(256 * z, 256 * z + 256)
-        n = jnp.concatenate([n_ref[:, cols], n_other_ref[:, cols]], axis=0)
-        for j, ref in enumerate((dq_ref, dk_ref, dv_ref)):
-            gqkv[j, z] = low(dot_tn(n, ref[...])).reshape(2, 2, 2, 32, 512)
+    plan = term_plan(meta_ref, own, send_x, send_y, keep_a, keep_b, gqkv, go)
+    copies = [pltpu.make_async_copy(a, b, sems.at[k]) for k, (a, b) in enumerate(plan)]
+
+    def leave(weight):
+        for k, copy in enumerate(copies):
+            if (k % 8 % 3 if k % 8 < 6 else 3) == weight:
+                copy.start()
+
+    columns = [slice(256 * z, 256 * z + 256) for z in range(4)]
+    n = [jnp.concatenate([n_ref[:, cols], n_other_ref[:, cols]], axis=0) for cols in columns]
+    for j, ref in enumerate((dq_ref, dk_ref, dv_ref)):
+        for z in range(4):
+            gqkv[j, z] = low(dot_tn(n[z], ref[...])).reshape(2, 2, 2, 32, 512)
+        leave(j)
     grad = jnp.concatenate([g_ref[...], g_other_ref[...]], axis=0)
     for z in range(4):
         term = low(dot_tn(m_ref[:, 128 * z : 128 * z + 128], grad))
         for h in range(2):
             go[h, z] = term[:, 512 * h : 512 * h + 512].reshape(2, 2, 32, 512)
-    run_copies(term_plan(meta_ref, own, send_x, send_y, keep_a, keep_b, gqkv, go), sems)
+    leave(3)
+    for copy in copies:
+        copy.wait()
 
 
 def ffn_plan(both, wu, wd):

time: 275 us -> 275 us (level)
  no operation moved by 1% of the time
where the time goes in v2:
time: 275 us; the launch traced here: 273 us
  Pallas kernels  120 us (44%)
  waiting for transfers between devices  63.9 us (23%)
  starting transfers between devices  59.9 us (22%)
  between operations  14.5 us (5%)
  local copies, waits for them, and re-layouts  12.1 us (4%)
    pallas_call x19, Pallas kernels, whole_call(): pl.pallas_call(body, in_specs=[HBM if sp is None else sp for sp in in_spe...  74.3 us
    ppermute x36, waiting for transfers between devices, swap(): return lax.ppermute(v, axis, [(0, 1), (1, 0)])  48.6 us
    pallas_call x3, Pallas kernels, conv_call(): pl.pallas_call(body, grid_spec=pltpu.PrefetchScalarGridSpec(num_scalar_pr...  34.6 us
    ppermute x36, starting transfers between devices, swap(): return lax.ppermute(v, axis, [(0, 1), (1, 0)])  26.2 us
    all_to_all x1, waiting for transfers between devices, local(): got = lax.all_to_all(payload, groups, 0, 0, tiled=True)  7.74 us
    all_to_all x1, starting transfers between devices, local(): got = lax.all_to_all(payload, groups, 0, 0, tiled=True)  7.18 us
    unnamed x64, local copies, waits for them, and re-layouts  6.72 us
    ppermute x4, starting transfers between devices, swap_across(): return lax.ppermute(v, ('y', 'x'), [(i, 3 - i) for i in range(4)])  6.33 us
  transfers between devices with their start and end apart: 50, of which 24 were waited for; matrix products, arithmetic and copies ran while one was open for 3% of the time, Pallas kernels for 33%

profile of v2, /device:TPU:0, one launch (start us, length us, event | category | flops | bytes accessed | tf_op | source)
XLA Modules:
  0.0 273.3 jit_solution(2144387257145634361)
XLA Ops:
  13.7 2.9 %collective-permute-start.1 = (bf16[128,1024]{1,0:T(8,128)(2,1)S(1)}, bf16[128,1024]{1,0:T(8,128)(2,1)S(1)}, u32[]{:S(2)}, u32[]{:S(2)}) collective-permute-start(bf16[128,1024]{1,0:T(8,128)(2,1)S(1)} %get-tuple-element.86.refs_0_), channel_id=1, source_target_pairs={{0,4},{4,0},{1,5},{5,1},{2,6},{6,2},{3,7},{7,3},{8,12},{12,8},{9,1... | collective-permute-start | bytes 786440 | tf_op jit(solution)/shard_map/ppermute | solution.py:1170
  16.6 3.4 %all-to-all-start.2 = ((bf16[8,32,512]{2,1,0:T(8,128)(2,1)}), bf16[8,32,512]{2,1,0:T(8,128)(2,1)S(1)}, u32[]{:S(2)}, u32[]{:S(2)}) async-start(bf16[8,32,512]{2,1,0:T(8,128)(2,1)} %get-tuple-element.94), calls=%async_computation.2 | async-start | bytes 524288 | tf_op jit(solution)/shard_map/all_to_all | solution.py:1220
  26.6 7.2 %all-to-all-start = ((bf16[16,80,128]{2,1,0:T(8,128)(2,1)}), bf16[16,80,128]{2,1,0:T(8,128)(2,1)S(1)}, u32[]{:S(2)}, u32[]{:S(2)}) async-start(bf16[16,80,128]{2,1,0:T(8,128)(2,1)} %shard_map.341), calls=%async_computation | async-start | bytes 655360 | tf_op jit(solution)/shard_map/all_to_all | solution.py:1223
  34.3 2.9 %collective-permute-done.2.refs_1_.refs_4_ = bf16[32,8192]{1,0:T(8,128)(2,1)S(1)} collective-permute-done((bf16[32,8192]{1,0:T(8,128)(2,1)S(1)}, bf16[32,8192]{1,0:T(8,128)(2,1)S(1)}, u32[]{:S(2)}, u32[]{:S(2)}) %collective-permute-start.2) | collective-permute-done | bytes 524320 | tf_op jit(solution)/shard_map/ppermute | solution.py:1170
  39.3 2.6 collective-permute-start.5
  42.0 7.7 %all-to-all-done.refs_2_ = bf16[16,80,128]{2,1,0:T(8,128)(2,1)S(1)} async-done(((bf16[16,80,128]{2,1,0:T(8,128)(2,1)}), bf16[16,80,128]{2,1,0:T(8,128)(2,1)S(1)}, u32[]{:S(2)}, u32[]{:S(2)}) %all-to-all-start) | async-done | bytes 327712 | tf_op jit(solution)/shard_map/all_to_all | solution.py:1223
  51.9 10.0 %shard_map.343.refs_3_ = bf16[16,64,128]{2,1,0:T(8,128)(2,1)} custom-call(s32[64]{0:T(128)S(1)} %reshape.58.refs_0_.refs_1_, s32[4]{0:T(128)S(1)} %pad_add_fusion.refs_1_.refs_0_, bf16[16,80,128]{2,1,0:T(8,128)(2,1)S(1)} %all-to-all-done.refs_2_, bf16[32,8192]{1,0:T(8,128)(2,1)} %refs_3_.5, bf16[32,8192]{1,0:T(8,128)(2,1)} %copy-done.14, ...), custom_call_target="tpu_custom_call" | custom-call | flops 30000001024 | bytes 1024 | tf_op jit(solution)/shard_map/pallas_call | solution.py:739
  61.9 3.7 %all-to-all-start.1 = ((bf16[16,64,128]{2,1,0:T(8,128)(2,1)}), bf16[16,64,128]{2,1,0:T(8,128)(2,1)S(1)}, u32[]{:S(2)}, u32[]{:S(2)}) async-start(bf16[16,64,128]{2,1,0:T(8,128)(2,1)} %shard_map.343.refs_3_), calls=%async_computation.1 | async-start | bytes 524288 | tf_op jit(solution)/shard_map/all_to_all | solution.py:1230
  66.1 9.4 %collective-permute-done.10.refs_8_.refs_5_ = bf16[4,8,32,512]{3,2,1,0:T(8,128)(2,1)S(1)} collective-permute-done((bf16[4,8,32,512]{3,2,1,0:T(8,128)(2,1)}, bf16[4,8,32,512]{3,2,1,0:T(8,128)(2,1)S(1)}, u32[]{:S(2)}, u32[]{:S(2)}) %collective-permute-start.10) | collective-permute-done | bytes 1048608 | tf_op jit(solution)/shard_map/ppermute | solution.py:1170
  83.3 2.7 shard_map.345
  87.5 5.9 %collective-permute-done.13.refs_7_.refs_10_ = bf16[2,8,32,512]{3,2,1,0:T(8,128)(2,1)} collective-permute-done((bf16[2,8,32,512]{3,2,1,0:T(8,128)(2,1)}, bf16[2,8,32,512]{3,2,1,0:T(8,128)(2,1)}, u32[]{:S(2)}, u32[]{:S(2)}) %collective-permute-start.13) | collective-permute-done | bytes 524320 | tf_op jit(solution)/shard_map/ppermute | solution.py:1170
  94.2 9.5 %shard_map.346 = (bf16[256,512]{1,0:T(8,128)(2,1)}, bf16[256,512]{1,0:T(8,128)(2,1)}, bf16[256,512]{1,0:T(8,128)(2,1)}, bf16[256,512]{1,0:T(8,128)(2,1)}, f32[12...) custom-call(s32[4]{0:T(128)S(1)} %pad_add_fusion.refs_1_.refs_0_, s32[64]{0:T(128)S(1)} %reshape.58.refs_0_.refs_1_, ...), custom_call_target="tpu_custom_call" | custom-call | flops 8000000000 | bytes 1024 | tf_op jit(solution)/shard_map/pallas_call | solution.py:488
  109.7 5.7 %collective-permute-done.16.refs_1_.refs_10_ = bf16[128,1024]{1,0:T(8,128)(2,1)S(1)} collective-permute-done((bf16[128,1024]{1,0:T(8,128)(2,1)S(1)}, bf16[128,1024]{1,0:T(8,128)(2,1)S(1)}, u32[]{:S(2)}, u32[]{:S(2)}) %collective-permute-start.16) | collective-permute-done | bytes 262176 | tf_op jit(solution)/shard_map/ppermute | solution.py:1170
  115.9 4.7 %collective-permute-done.18.refs_3_.refs_12_ = bf16[128,1024]{1,0:T(8,128)(2,1)S(1)} collective-permute-done((bf16[128,1024]{1,0:T(8,128)(2,1)S(1)}, bf16[128,1024]{1,0:T(8,128)(2,1)S(1)}, u32[]{:S(2)}, u32[]{:S(2)}) %collective-permute-start.18) | collective-permute-done | bytes 262176 | tf_op jit(solution)/shard_map/ppermute | solution.py:1174
  122.9 10.2 %shard_map.348 = (bf16[1024,512]{1,0:T(8,128)(2,1)S(1)}, bf16[1024,512]{1,0:T(8,128)(2,1)S(1)}, f32[512,1024]{1,0:T(8,128)S(1)}, bf16[512,1024]{1,0:T(8,128)(2,1)S(1)}, f32[1,512]{1,0:T(1,128)S(1)}) custom-call(bf16[128,1024]{1,0:T(8,128)(2,1)S(1)} %get-tuple-element.96.refs_0_.refs_9_, bf16[128,1024]{1,0:T(8,128)(2,1)} %copy-done.24, ...), custom_call_target="tpu_custom_call" | custom-call | flops 30000001024 | bytes 1024 | tf_op jit(solution)/shard_map/pallas_call | solution.py:488
  140.2 6.1 %shard_map.351.refs_7_ = bf16[4,512,512]{2,1,0:T(8,128)(2,1)} custom-call(bf16[1024,512]{1,0:T(8,128)(2,1)S(1)} %get-tuple-element.98.refs_0_, bf16[128,1024]{1,0:T(8,128)(2,1)S(1)} %get-tuple-element.88.refs_8_.refs_1_.refs_5_, bf16[128,1024]{1,0:T(8,128)(2,1)} %collective-permute-done.3.refs_6_.refs_9_.refs_2_, bf16[128,1024]{1,0:T(8,128)(2,1)} %copy-done.15, ...), custom_call_target="tpu_custom_call" | custom-call | flops 20000000000 | bytes 1024 | tf_op jit(solution)/shard_map/pallas_call | solution.py:1093
  146.4 4.7 %shard_map.350 = (f32[512,1024]{1,0:T(8,128)}, bf16[512,1024]{1,0:T(8,128)(2,1)}) custom-call(bf16[1024,512]{1,0:T(8,128)(2,1)} %copy-done.6, bf16[4,512,512]{2,1,0:T(8,128)(2,1)} %bitcast.34, bf16[128,1024]{1,0:T(8,128)(2,1)S(1)} %get-tuple-element.101.refs_2_.refs_18_), custom_call_target="tpu_custom_call" | custom-call | flops 1000000000 | bytes 1024 | tf_op jit(solution)/shard_map/pallas_call | solution.py:488
  155.6 11.6 %shard_map.353 = (bf16[256,512]{1,0:T(8,128)(2,1)S(1)}, bf16[256,512]{1,0:T(8,128)(2,1)S(1)}, bf16[256,512]{1,0:T(8,128)(2,1)S(1)}, f32[2,512]{1,0:T(2,128)S(1)}...) custom-call(s32[4]{0:T(128)S(1)} %pad_add_fusion.refs_1_.refs_0_, s32[64]{0:T(128)S(1)} %reshape.58.refs_0_.refs_1_, ...), custom_call_target="tpu_custom_call" | custom-call | flops 70000001024 | bytes 1024 | tf_op jit(solution)/shard_map/pallas_call | solution.py:488
  168.9 5.0 %shard_map.354 = (f32[128,1024]{1,0:T(8,128)}, bf16[16,80,128]{2,1,0:T(8,128)(2,1)}) custom-call(s32[4]{0:T(128)S(1)} %pad_add_fusion.refs_1_.refs_0_, f32[128,1024]{1,0:T(8,128)S(1)} %get-tuple-element.112.refs_1_, bf16[128,1024]{1,0:T(8,128)(2,1)S(1)} %collective-permute-done.29.refs_2_, f32[128,1024]{1,0:T(8,128)} %get-tuple-element.114.refs_3_, ...), custom_call_target="tpu_custom_call" | custom-call | flops 10000000000 | bytes 1024 | tf_op jit(solution)/shard_map/pallas_call | solution.py:488
  174.0 5.0 %all-to-all-start.3 = ((bf16[16,80,128]{2,1,0:T(8,128)(2,1)}), bf16[16,80,128]{2,1,0:T(8,128)(2,1)S(1)}, u32[]{:S(2)}, u32[]{:S(2)}) async-start(bf16[16,80,128]{2,1,0:T(8,128)(2,1)} %get-tuple-element.120.refs_2_.refs_9_), calls=%async_computation.3 | async-start | bytes 655360 | tf_op jit(solution)/shard_map/all_to_all | solution.py:1293
  179.7 5.1 %shard_map.356 = (bf16[4,8,32,512]{3,2,1,0:T(8,128)(2,1)}, bf16[2,4,4,32,512]{4,3,2,1,0:T(8,128)(2,1)}, bf16[2,4,4,32,512]{4,3,2,1,0:T(8,128)(2,1)}, bf16[4,4,32...) custom-call(s32[4]{0:T(128)S(1)} %pad_add_fusion.refs_1_.refs_0_, bf16[128,1024]{1,0:T(8,128)(2,1)S(1)} %get-tuple-element.90.refs_2_.refs_1_, ...), custom_call_target="tpu_custom_call" | custom-call | flops 1000000000 | bytes 1024 | tf_op jit(solution)/shard_map/pallas_call | solution.py:488
  187.5 3.3 %shard_map.355 = (f32[128,1024]{1,0:T(8,128)}, bf16[128,1024]{1,0:T(8,128)(2,1)S(1)}, bf16[128,1024]{1,0:T(8,128)(2,1)S(1)}, bf16[128,1024]{1,0:T(8,128)(2,1)S(1)}) custom-call(f32[512,1024]{1,0:T(8,128)} %get-tuple-element.102.refs_0_, bf16[512,1024]{1,0:T(8,128)(2,1)S(1)} %collective-permute-done.24.refs_1_, ...), custom_call_target="tpu_custom_call" | custom-call | flops 50000000 | bytes 1024 | tf_op jit(solution)/shard_map/pallas_call | solution.py:488
  192.3 11.3 %shard_map.357.refs_0_.refs_4_ = bf16[16,64,128]{2,1,0:T(8,128)(2,1)} custom-call(s32[64]{0:T(128)S(1)} %reshape.58.refs_0_.refs_1_, s32[4]{0:T(128)S(1)} %pad_add_fusion.refs_1_.refs_0_, bf16[16,80,128]{2,1,0:T(8,128)(2,1)S(1)} %all-to-all-done.3.refs_2_.refs_3_, bf16[32,8192]{1,0:T(8,128)(2,1)} %refs_3_.5, bf16[32,8192]{1,0:T(8,128)(2,1)} %copy-done.14, ...), custom_call_target="tpu_custom_call" | custom-call | flops 10000000000 | bytes 1024 | tf_op jit(solution)/shard_map/pallas_call | solution.py:739
  203.6 4.4 %all-to-all-start.4 = ((bf16[16,64,128]{2,1,0:T(8,128)(2,1)}), bf16[16,64,128]{2,1,0:T(8,128)(2,1)S(1)}, u32[]{:S(2)}, u32[]{:S(2)}) async-start(bf16[16,64,128]{2,1,0:T(8,128)(2,1)} %shard_map.357.refs_0_.refs_4_), calls=%async_computation.4 | async-start | bytes 524288 | tf_op jit(solution)/shard_map/all_to_all | solution.py:1306
  208.0 2.6 collective-permute-done.30.x_ref
  217.0 13.3 %shard_map.362 = (f32[32,8192]{1,0:T(8,128)}, bf16[32,8192]{1,0:T(8,128)(2,1)}) custom-call(s32[64]{0:T(128)S(1)} %reshape.58.refs_0_.refs_1_, s32[4]{0:T(128)S(1)} %pad_add_fusion.refs_1_.refs_0_, bf16[16,80,128]{2,1,0:T(8,128)(2,1)S(1)} %copy-done.1, bf16[16,80,128]{2,1,0:T(8,128)(2,1)S(1)} %all-to-all-done.3.refs_2_.refs_3_, ...), custom_call_target="tpu_custom_call" | custom-call | flops 30000001024 | bytes 1024 | tf_op jit(solution)/shard_map/pallas_call | solution.py:739
  232.1 2.8 %shard_map.363.refs_6_.refs_2_.refs_1_ = bf16[4,8,32,512]{3,2,1,0:T(8,128)(2,1)} custom-call(bf16[4,8,32,512]{3,2,1,0:T(8,128)(2,1)} %get-tuple-element.134.own_ref, bf16[2,4,4,32,512]{4,3,2,1,0:T(8,128)(2,1)} %collective-permute-done.30.x_ref, bf16[2,4,4,32,512]{4,3,2,1,0:T(8,128)(2,1)} %collective-permute-done.31.y_ref, ...), custom_call_target="tpu_custom_call" | custom-call | flops 3000000000 | bytes 1024 | tf_op jit(solution)/shard_map/pallas_call | solution.py:1131
  240.5 5.1 %collective-permute-done.38 = f32[16,32]{1,0:T(8,128)S(1)} collective-permute-done((f32[16,32]{1,0:T(8,128)}, f32[16,32]{1,0:T(8,128)S(1)}, u32[]{:S(2)}, u32[]{:S(2)}) %collective-permute-start.38) | collective-permute-done | bytes 2080 | tf_op jit(solution)/shard_map/ppermute | solution.py:1170
  247.8 3.4 %all-to-all-start.5 = ((bf16[8,32,512]{2,1,0:T(8,128)(2,1)}), bf16[8,32,512]{2,1,0:T(8,128)(2,1)S(1)}, u32[]{:S(2)}, u32[]{:S(2)}) async-start(bf16[8,32,512]{2,1,0:T(8,128)(2,1)} %bitcast.14), calls=%async_computation.7 | async-start | bytes 524288 | tf_op jit(solution)/shard_map/all_to_all | solution.py:1319
  252.3 2.6 shard_map.365.refs_5_
  257.6 2.6 shard_map.368
  263.8 2.9 %shard_map.370 = (f32[32,1024]{1,0:T(8,128)}, f32[32,1024]{1,0:T(8,128)}, f32[32,1024]{1,0:T(8,128)}, f32[32,1024]{1,0:T(8,128)}) custom-call(s32[4]{0:T(128)S(1)} %pad_add_fusion.refs_1_.refs_0_, bf16[8,32,512]{2,1,0:T(8,128)(2,1)} %shard_map.369.refs_1_, bf16[8,32,512]{2,1,0:T(8,128)(2,1)S(1)} %collective-permute-done.39.refs_2_), custom_call_target="tpu_custom_call" | custom-call | flops 50000000 | bytes 1024 | tf_op jit(solution)/shard_map/pallas_call | solution.py:488
  (186 shorter events, 78.3 us)
Async XLA Ops:
  7.2 42.6 %all-gather.5.cloned.1.call-start = ((), (), s32[]{:S(2)}) async-start(), calls=%async_computation.10 | async-start | bytes 1310720 | tf_op jit(solution)/shard_map/all_gather | solution.py:1178
  16.6 10.0 %all-to-all-start.2 = ((bf16[8,32,512]{2,1,0:T(8,128)(2,1)}), bf16[8,32,512]{2,1,0:T(8,128)(2,1)S(1)}, u32[]{:S(2)}, u32[]{:S(2)}) async-start(bf16[8,32,512]{2,1,0:T(8,128)(2,1)} %get-tuple-element.94), calls=%async_computation.2 | async-start | bytes 524288 | tf_op jit(solution)/shard_map/all_to_all | solution.py:1220
  20.1 17.2 %collective-permute-start.2 = (bf16[32,8192]{1,0:T(8,128)(2,1)S(1)}, bf16[32,8192]{1,0:T(8,128)(2,1)S(1)}, u32[]{:S(2)}, u32[]{:S(2)}) collective-permute-start(bf16[32,8192]{1,0:T(8,128)(2,1)S(1)} %copy-done.21), channel_id=1, source_target_pairs={{0,1},{1,0},{2,3},{3,2},{4,5},{5,4},{6,7},{7,6},{8,9},{9,8},{10,11... | collective-permute-start | bytes 1572872 | tf_op jit(solution)/shard_map/ppermute | solution.py:1170
  26.6 23.1 %all-to-all-start = ((bf16[16,80,128]{2,1,0:T(8,128)(2,1)}), bf16[16,80,128]{2,1,0:T(8,128)(2,1)S(1)}, u32[]{:S(2)}, u32[]{:S(2)}) async-start(bf16[16,80,128]{2,1,0:T(8,128)(2,1)} %shard_map.341), calls=%async_computation | async-start | bytes 655360 | tf_op jit(solution)/shard_map/all_to_all | solution.py:1223
  33.8 70.0 %all-gather.7.cloned.1.call-start = ((), (), s32[]{:S(2)}) async-start(), calls=%async_computation.11 | async-start | bytes 2621440 | tf_op jit(solution)/shard_map/all_gather | solution.py:1178
  33.9 45.0 %collective-permute-start.6 = (bf16[128,1024]{1,0:T(8,128)(2,1)S(1)}, bf16[128,1024]{1,0:T(8,128)(2,1)}, u32[]{:S(2)}, u32[]{:S(2)}) collective-permute-start(bf16[128,1024]{1,0:T(8,128)(2,1)S(1)} %get-tuple-element.88.refs_8_.refs_1_.refs_5_), channel_id=1, source_target_pairs={{0,2},{2,0},{1,3},{3,1},{4,6},{6,4},{5,7},{7,5},{8,10},{10,8},{9,1... | collective-permute-start | bytes 786440 | tf_op jit(solution)/shard_map/ppermute | solution.py:1170
  38.0 13.9 %collective-permute-start.3 = (bf16[128,1024]{1,0:T(8,128)(2,1)}, bf16[128,1024]{1,0:T(8,128)(2,1)}, u32[]{:S(2)}, u32[]{:S(2)}) collective-permute-start(bf16[128,1024]{1,0:T(8,128)(2,1)} %shard_map.342), channel_id=1, source_target_pairs={{0,1},{1,0},{2,3},{3,2},{4,5},{5,4},{6,7},{7,6},{8,9},{9,8},{10,11... | collective-permute-start | bytes 786440 | tf_op jit(solution)/shard_map/ppermute | solution.py:1170
  39.3 37.0 %collective-permute-start.5 = (bf16[128,1024]{1,0:T(8,128)(2,1)}, bf16[128,1024]{1,0:T(8,128)(2,1)}, u32[]{:S(2)}, u32[]{:S(2)}) collective-permute-start(bf16[128,1024]{1,0:T(8,128)(2,1)} %shard_map.342), channel_id=1, source_target_pairs={{0,5},{1,4},{4,1},{5,0},{2,7},{3,6},{6,3},{7,2},{8,13},{9,12},{12,... | collective-permute-start | bytes 786440 | tf_op jit(solution)/shard_map/ppermute | solution.py:1174
  49.9 25.5 %collective-permute-start.10 = (bf16[4,8,32,512]{3,2,1,0:T(8,128)(2,1)}, bf16[4,8,32,512]{3,2,1,0:T(8,128)(2,1)S(1)}, u32[]{:S(2)}, u32[]{:S(2)}) collective-permute-start(bf16[4,8,32,512]{3,2,1,0:T(8,128)(2,1)} %bitcast.39), channel_id=1, source_target_pairs={{0,1},{1,0},{2,3},{3,2},{4,5},{5,4},{6,7},{7,6},{8,9},{9,8},{10,11... | collective-permute-start | bytes 3145736 | tf_op jit(solution)/shard_map/ppermute | solution.py:1170
  51.6 26.3 %collective-permute-start.11 = (bf16[4,8,32,512]{3,2,1,0:T(8,128)(2,1)}, bf16[4,8,32,512]{3,2,1,0:T(8,128)(2,1)S(1)}, u32[]{:S(2)}, u32[]{:S(2)}) collective-permute-start(bf16[4,8,32,512]{3,2,1,0:T(8,128)(2,1)} %bitcast.40), channel_id=1, source_target_pairs={{0,4},{4,0},{1,5},{5,1},{2,6},{6,2},{3,7},{7,3},{8,12},{12,8},{9,1... | collective-permute-start | bytes 3145736 | tf_op jit(solution)/shard_map/ppermute | solution.py:1170
  61.9 21.4 %all-to-all-start.1 = ((bf16[16,64,128]{2,1,0:T(8,128)(2,1)}), bf16[16,64,128]{2,1,0:T(8,128)(2,1)S(1)}, u32[]{:S(2)}, u32[]{:S(2)}) async-start(bf16[16,64,128]{2,1,0:T(8,128)(2,1)} %shard_map.343.refs_3_), calls=%async_computation.1 | async-start | bytes 524288 | tf_op jit(solution)/shard_map/all_to_all | solution.py:1230
  65.6 14.2 %collective-permute-start.4 = (bf16[16,16,128]{2,1,0:T(8,128)(2,1)S(1)}, bf16[16,16,128]{2,1,0:T(8,128)(2,1)S(1)}, u32[]{:S(2)}, u32[]{:S(2)}) collective-permute-start(bf16[16,16,128]{2,1,0:T(8,128)(2,1)S(1)} %slice.73.refs_1_), channel_id=1, source_target_pairs={{0,1},{1,0},{2,3},{3,2},{4,5},{5,4},{6,7},{7,6},{8,9},{9,8},{10,11... | collective-permute-start | bytes 196616 | tf_op jit(solution)/shard_map/ppermute | solution.py:1170
  78.9 14.6 %collective-permute-start.13 = (bf16[2,8,32,512]{3,2,1,0:T(8,128)(2,1)}, bf16[2,8,32,512]{3,2,1,0:T(8,128)(2,1)}, u32[]{:S(2)}, u32[]{:S(2)}) collective-permute-start(bf16[2,8,32,512]{3,2,1,0:T(8,128)(2,1)} %slice.74), channel_id=1, source_target_pairs={{0,4},{4,0},{1,5},{5,1},{2,6},{6,2},{3,7},{7,3},{8,12},{12,8},{9,1... | collective-permute-start | bytes 1572872 | tf_op jit(solution)/shard_map/ppermute | solution.py:1170
  79.9 14.3 %collective-permute-start.14 = (bf16[2,8,32,512]{3,2,1,0:T(8,128)(2,1)}, bf16[2,8,32,512]{3,2,1,0:T(8,128)(2,1)}, u32[]{:S(2)}, u32[]{:S(2)}) collective-permute-start(bf16[2,8,32,512]{3,2,1,0:T(8,128)(2,1)} %slice.75), channel_id=1, source_target_pairs={{0,1},{1,0},{2,3},{3,2},{4,5},{5,4},{6,7},{7,6},{8,9},{9,8},{10,11... | collective-permute-start | bytes 1572872 | tf_op jit(solution)/shard_map/ppermute | solution.py:1170
  107.8 12.8 %collective-permute-start.18 = (bf16[128,1024]{1,0:T(8,128)(2,1)S(1)}, bf16[128,1024]{1,0:T(8,128)(2,1)S(1)}, u32[]{:S(2)}, u32[]{:S(2)}) collective-permute-start(bf16[128,1024]{1,0:T(8,128)(2,1)S(1)} %get-tuple-element.96.refs_0_.refs_9_), channel_id=1, source_target_pairs={{0,5},{1,4},{4,1},{5,0},{2,7},{3,6},{6,3},{7,2},{8,13},{9,12},{12,... | collective-permute-start | bytes 786440 | tf_op jit(solution)/shard_map/ppermute | solution.py:1174
  109.7 10.9 %collective-permute-start.19 = (bf16[128,1024]{1,0:T(8,128)(2,1)S(1)}, bf16[128,1024]{1,0:T(8,128)(2,1)S(1)}, u32[]{:S(2)}, u32[]{:S(2)}) collective-permute-start(bf16[128,1024]{1,0:T(8,128)(2,1)S(1)} %get-tuple-element.96.refs_0_.refs_9_), channel_id=1, source_target_pairs={{0,2},{2,0},{1,3},{3,1},{4,6},{6,4},{5,7},{7,5},{8,10},{10,8},{9,1... | collective-permute-start | bytes 786440 | tf_op jit(solution)/shard_map/ppermute | solution.py:1170
  136.6 14.5 %collective-permute-start.25 = (bf16[128,1024]{1,0:T(8,128)(2,1)S(1)}, bf16[128,1024]{1,0:T(8,128)(2,1)S(1)}, u32[]{:S(2)}, u32[]{:S(2)}) collective-permute-start(bf16[128,1024]{1,0:T(8,128)(2,1)S(1)} %get-tuple-element.101.refs_2_.refs_18_), channel_id=1, source_target_pairs={{0,1},{1,0},{2,3},{3,2},{4,5},{5,4},{6,7},{7,6},{8,9},{9,8},{10,11... | collective-permute-start | bytes 786440 | tf_op jit(solution)/shard_map/ppermute | solution.py:1170
  138.4 13.7 %collective-permute-start.26 = (bf16[128,1024]{1,0:T(8,128)(2,1)S(1)}, bf16[128,1024]{1,0:T(8,128)(2,1)S(1)}, u32[]{:S(2)}, u32[]{:S(2)}) collective-permute-start(bf16[128,1024]{1,0:T(8,128)(2,1)S(1)} %get-tuple-element.105), channel_id=1, source_target_pairs={{0,4},{4,0},{1,5},{5,1},{2,6},{6,2},{3,7},{7,3},{8,12},{12,8},{9,1... | collective-permute-start | bytes 786440 | tf_op jit(solution)/shard_map/ppermute | solution.py:1170
  139.4 12.7 %collective-permute-start.27 = (bf16[128,1024]{1,0:T(8,128)(2,1)S(1)}, bf16[128,1024]{1,0:T(8,128)(2,1)S(1)}, u32[]{:S(2)}, u32[]{:S(2)}) collective-permute-start(bf16[128,1024]{1,0:T(8,128)(2,1)S(1)} %get-tuple-element.106), channel_id=1, source_target_pairs={{0,5},{1,4},{4,1},{5,0},{2,7},{3,6},{6,3},{7,2},{8,13},{9,12},{12,... | collective-permute-start | bytes 786440 | tf_op jit(solution)/shard_map/ppermute | solution.py:1174
  167.5 20.0 %collective-permute-start.24 = (bf16[512,1024]{1,0:T(8,128)(2,1)}, bf16[512,1024]{1,0:T(8,128)(2,1)S(1)}, u32[]{:S(2)}, u32[]{:S(2)}) collective-permute-start(bf16[512,1024]{1,0:T(8,128)(2,1)} %get-tuple-element.103.refs_8_), channel_id=1, source_target_pairs={{0,2},{2,0},{1,3},{3,1},{4,6},{6,4},{5,7},{7,5},{8,10},{10,8},{9,1... | collective-permute-start | bytes 3145736 | tf_op jit(solution)/shard_map/ppermute | solution.py:1170
  174.0 18.3 %all-to-all-start.3 = ((bf16[16,80,128]{2,1,0:T(8,128)(2,1)}), bf16[16,80,128]{2,1,0:T(8,128)(2,1)S(1)}, u32[]{:S(2)}, u32[]{:S(2)}) async-start(bf16[16,80,128]{2,1,0:T(8,128)(2,1)} %get-tuple-element.120.refs_2_.refs_9_), calls=%async_computation.3 | async-start | bytes 655360 | tf_op jit(solution)/shard_map/all_to_all | solution.py:1293
  179.0 52.1 %reduce-scatter.3.cloned.1.call-start = ((), (), s32[]{:S(2)}) async-start(), calls=%async_computation.8 | async-start | bytes 2621440 | tf_op jit(solution)/shard_map/reduce_scatter | solution.py:1182
  184.8 25.9 %collective-permute-start.30 = (bf16[2,4,4,32,512]{4,3,2,1,0:T(8,128)(2,1)}, bf16[2,4,4,32,512]{4,3,2,1,0:T(8,128)(2,1)}, u32[]{:S(2)}, u32[]{:S(2)}) collective-permute-start(bf16[2,4,4,32,512]{4,3,2,1,0:T(8,128)(2,1)} %get-tuple-element.129), channel_id=1, source_target_pairs={{0,1},{1,0},{2,3},{3,2},{4,5},{5,4},{6,7},{7,6},{8,9},{9,8},{10,11... | collective-permute-start | bytes 3145736 | tf_op jit(solution)/shard_map/ppermute | solution.py:1170
  185.6 26.5 %collective-permute-start.31 = (bf16[2,4,4,32,512]{4,3,2,1,0:T(8,128)(2,1)}, bf16[2,4,4,32,512]{4,3,2,1,0:T(8,128)(2,1)}, u32[]{:S(2)}, u32[]{:S(2)}) collective-permute-start(bf16[2,4,4,32,512]{4,3,2,1,0:T(8,128)(2,1)} %get-tuple-element.130), channel_id=1, source_target_pairs={{0,4},{4,0},{1,5},{5,1},{2,6},{6,2},{3,7},{7,3},{8,12},{12,8},{9,1... | collective-permute-start | bytes 3145736 | tf_op jit(solution)/shard_map/ppermute | solution.py:1170
  203.6 27.5 %all-to-all-start.4 = ((bf16[16,64,128]{2,1,0:T(8,128)(2,1)}), bf16[16,64,128]{2,1,0:T(8,128)(2,1)S(1)}, u32[]{:S(2)}, u32[]{:S(2)}) async-start(bf16[16,64,128]{2,1,0:T(8,128)(2,1)} %shard_map.357.refs_0_.refs_4_), calls=%async_computation.4 | async-start | bytes 524288 | tf_op jit(solution)/shard_map/all_to_all | solution.py:1306
  208.0 54.1 %reduce-scatter.5.cloned.1.call-start = ((), (), s32[]{:S(2)}) async-start(), calls=%async_computation.9 | async-start | bytes 1310720 | tf_op jit(solution)/shard_map/reduce_scatter | solution.py:1182
  214.6 16.5 %collective-permute-start.35 = (bf16[4,4,32,512]{3,2,1,0:T(8,128)(2,1)}, bf16[4,4,32,512]{3,2,1,0:T(8,128)(2,1)S(1)}, u32[]{:S(2)}, u32[]{:S(2)}) collective-permute-start(bf16[4,4,32,512]{3,2,1,0:T(8,128)(2,1)} %get-tuple-element.135.refs_1_), channel_id=1, source_target_pairs={{0,4},{4,0},{1,5},{5,1},{2,6},{6,2},{3,7},{7,3},{8,12},{12,8},{9,1... | collective-permute-start | bytes 1572872 | tf_op jit(solution)/shard_map/ppermute | solution.py:1170
  215.8 15.3 %collective-permute-start.36 = (bf16[4,4,32,512]{3,2,1,0:T(8,128)(2,1)}, bf16[4,4,32,512]{3,2,1,0:T(8,128)(2,1)S(1)}, u32[]{:S(2)}, u32[]{:S(2)}) collective-permute-start(bf16[4,4,32,512]{3,2,1,0:T(8,128)(2,1)} %get-tuple-element.131.refs_1_), channel_id=1, source_target_pairs={{0,1},{1,0},{2,3},{3,2},{4,5},{5,4},{6,7},{7,6},{8,9},{9,8},{10,11... | collective-permute-start | bytes 1572872 | tf_op jit(solution)/shard_map/ppermute | solution.py:1170
  230.3 20.9 %collective-permute-start.37 = (bf16[32,8192]{1,0:T(8,128)(2,1)}, bf16[32,8192]{1,0:T(8,128)(2,1)S(1)}, u32[]{:S(2)}, u32[]{:S(2)}) collective-permute-start(bf16[32,8192]{1,0:T(8,128)(2,1)} %get-tuple-element.136.refs_0_), channel_id=1, source_target_pairs={{0,1},{1,0},{2,3},{3,2},{4,5},{5,4},{6,7},{7,6},{8,9},{9,8},{10,11... | collective-permute-start | bytes 1572872 | tf_op jit(solution)/shard_map/ppermute | solution.py:1170
  237.0 17.9 %collective-permute-start.34 = (bf16[128,1024]{1,0:T(8,128)(2,1)}, bf16[128,1024]{1,0:T(8,128)(2,1)S(1)}, u32[]{:S(2)}, u32[]{:S(2)}) collective-permute-start(bf16[128,1024]{1,0:T(8,128)(2,1)} %shard_map.361), channel_id=1, source_target_pairs={{0,5},{1,4},{4,1},{5,0},{2,7},{3,6},{6,3},{7,2},{8,13},{9,12},{12,... | collective-permute-start | bytes 786440 | tf_op jit(solution)/shard_map/ppermute | solution.py:1174
  238.0 16.9 %collective-permute-start.33 = (bf16[128,1024]{1,0:T(8,128)(2,1)}, bf16[128,1024]{1,0:T(8,128)(2,1)S(1)}, u32[]{:S(2)}, u32[]{:S(2)}) collective-permute-start(bf16[128,1024]{1,0:T(8,128)(2,1)} %shard_map.360), channel_id=1, source_target_pairs={{0,4},{4,0},{1,5},{5,1},{2,6},{6,2},{3,7},{7,3},{8,12},{12,8},{9,1... | collective-permute-start | bytes 786440 | tf_op jit(solution)/shard_map/ppermute | solution.py:1170
  239.2 15.8 %collective-permute-start.32 = (bf16[128,1024]{1,0:T(8,128)(2,1)}, bf16[128,1024]{1,0:T(8,128)(2,1)S(1)}, u32[]{:S(2)}, u32[]{:S(2)}) collective-permute-start(bf16[128,1024]{1,0:T(8,128)(2,1)} %shard_map.359), channel_id=1, source_target_pairs={{0,1},{1,0},{2,3},{3,2},{4,5},{5,4},{6,7},{7,6},{8,9},{9,8},{10,11... | collective-permute-start | bytes 786440 | tf_op jit(solution)/shard_map/ppermute | solution.py:1170
  (49 other events, 290.9 us)
Sparse Core Ops, SparseCore 0:
  11.4 36.7 all-gather.4
  49.8 49.9 all-gather.6
  182.1 48.6 reduce-scatter.2
  235.1 26.9 reduce-scatter.4
